TPU v7x, 1024 devices: a whole 4x4x32 slice. The times are simulated.
1024 devices in a mesh: graph: 128 (over z, x), feat: 8 (over y, core).
Axes of the slice: x: 4, y: 4, z: 32, core: 2. Of those that a mesh axis runs over, the one named last changes fastest.
Arguments:
- features: bfloat16 [128, 1048576], P('feat', 'graph'), may hold values from -6 to 6
- w_self: bfloat16 [128, 128], replicated, may hold values from -0.5 to 0.5
- w_neigh: bfloat16 [128, 128], replicated, may hold values from -0.5 to 0.5
- bias: float32 [128], replicated, may hold values from -3 to 3
- hub_pick: int32 [256], P('graph'), may hold values from 0 to 63
- halo_send: int32 [2048], P('graph'), may hold values from 0 to 63
- tile_dst: int32 [32768], P('graph'), may hold values from 0 to 63
- tile_src: int32 [32768], P('graph'), may hold values from 0 to 335, as said below
- tile_edges: int32 [32768], P('graph'), may hold values from 1 to 128, as said below
- tile_count: int32 [128], P('graph'), may hold values from 64 to 256, as said below
- edge_src: int32 [32768, 128], P('graph'), may hold values from 0 to 127
- edge_dst: int32 [32768, 128], P('graph'), may hold values from 0 to 127
Outputs:
- updated: bfloat16 [128, 1048576], P('feat', 'graph')
Inputs may be any that keep to these rules, and one draw needn't show every extreme that they name: `tile_src`: A tile's source index counts into table_p: below 64 own blocks, then 256 hub blocks, then 2 * 8 halo blocks; the largest value occurs in every draw. `tile_edges`: some tile of every draw has all 128 slots live. `tile_count`: some partition of every draw has all 256 tiles live.
All inputs are finite; a program needn't handle non-finite values.
Results may differ from a plain program's by a relative error of at most 0.0015.
Values may be sent and summed in bfloat16 or wider, within the bound.
No kernel may reach another device: no remote copies, remote signals or barrier semaphores. Data moves between devices by JAX's collectives and lax.ppermute only.
A program may use at most 64 MiB of HBM per device.

v0:
```python
import jax
import jax.numpy as jnp
from jax import lax
from jax.sharding import PartitionSpec as P

BLOCK = 128


def with_halo(block, sides, width):
    for axis, dim in sides:
        count = lax.axis_size(axis)
        forward = [(i, i + 1) for i in range(count - 1)]
        forward.append((count - 1, 0))
        backward = [(target, source) for source, target in forward]
        low = lax.ppermute(
            lax.slice_in_dim(block, block.shape[dim] - width, None, axis=dim), axis, forward
        )
        high = lax.ppermute(lax.slice_in_dim(block, 0, width, axis=dim), axis, backward)
        block = jnp.concatenate([low, block, high], axis=dim)
    return block


def shards(
    features,
    w_self,
    w_neigh,
    bias,
    hub_pick,
    halo_send,
    tile_dst,
    tile_src,
    tile_edges,
    tile_count,
    edge_src,
    edge_dst,
):
    feat_rows = features.shape[0]
    block_count = features.shape[1] // BLOCK
    halo_width = halo_send.shape[0] // 2
    blocks = features.reshape(feat_rows, block_count, BLOCK)
    hub_local = blocks[:, hub_pick, :]
    hub_rows = lax.all_gather(hub_local, "graph", axis=1, tiled=True)
    outgoing = blocks[:, halo_send, :]
    padded = with_halo(outgoing, (("graph", 1),), halo_width)
    table = jnp.concatenate(
        [blocks, hub_rows, padded[:, :halo_width], padded[:, 3 * halo_width :]], axis=1
    )
    flat_table = table.reshape(feat_rows, table.shape[1] * BLOCK)
    tile_slots = tile_dst.shape[0]
    edge_slots = edge_src.shape[1]
    live = (jnp.arange(edge_slots, dtype=jnp.int32)[None, :] < tile_edges[:, None]) & (
        jnp.arange(tile_slots, dtype=jnp.int32)[:, None] < tile_count[0]
    )
    source = tile_src[:, None] * BLOCK + edge_src
    gathered = flat_table[:, source]
    gathered = jnp.where(live[None], gathered, jnp.zeros((), jnp.bfloat16))
    one_hot = (
        (edge_dst[:, :, None] == jnp.arange(BLOCK, dtype=jnp.int32)[None, None, :])
        & live[:, :, None]
    ).astype(jnp.bfloat16)
    tile_sums = jnp.einsum("fte,teb->ftb", gathered, one_hot, preferred_element_type=jnp.float32)
    tile_degree = jnp.sum(one_hot, axis=1, dtype=jnp.float32)
    sums = jnp.zeros((feat_rows, block_count, BLOCK), jnp.float32).at[:, tile_dst, :].add(tile_sums)
    degree = jnp.zeros((block_count, BLOCK), jnp.float32).at[tile_dst, :].add(tile_degree)
    mean = (sums / jnp.maximum(degree, 1.0)[None]).astype(jnp.bfloat16)
    own_means = mean.reshape(feat_rows, block_count * BLOCK)
    feat_start = lax.axis_index("feat") * feat_rows
    self_rows = lax.dynamic_slice_in_dim(w_self, feat_start, feat_rows, 0)
    neigh_rows = lax.dynamic_slice_in_dim(w_neigh, feat_start, feat_rows, 0)
    input_piece = lax.all_gather(features, "feat", axis=0, tiled=True)
    mean_piece = lax.all_gather(own_means, "feat", axis=0, tiled=True)
    total = jnp.dot(self_rows, input_piece, preferred_element_type=jnp.float32) + jnp.dot(
        neigh_rows, mean_piece, preferred_element_type=jnp.float32
    )
    bias_rows = lax.dynamic_slice_in_dim(bias, feat_start, feat_rows, 0)
    return jax.nn.relu(total + bias_rows[:, None]).astype(jnp.bfloat16)


def solution(mesh):
    in_specs = (
        P("feat", "graph"),
        P(),
        P(),
        P(),
        P("graph"),
        P("graph"),
        P("graph"),
        P("graph"),
        P("graph"),
        P("graph"),
        P("graph", None),
        P("graph", None),
    )
    out_specs = P("feat", "graph")
    return jax.shard_map(shards, mesh=mesh, in_specs=in_specs, out_specs=out_specs, check_vma=False)
```

profile of v0, /device:TPU:6, one launch (start us, length us, event | category | flops | bytes accessed | tf_op | source)
XLA Modules:
  0.0 476.4 jit_solution(18181955502696218857)
XLA Ops:
  6.5 1.0 copy_bitcast_fusion.1
  7.5 0.7 compare_select_fusion.3
  8.2 1.1 gather_fusion
  9.4 0.0 all-gather.9.cloned.1.call-update
  9.4 0.0 all-gather.5.cloned.1.call-start
  9.4 0.7 compare_select_fusion.2
  10.1 0.6 gather_fusion.1
  10.7 3.7 collective-permute-start
  14.4 2.1 collective-permute-start.1
  16.6 0.0 all-gather.5.cloned.1.call-update
  16.6 0.0 all-gather.7.cloned.1.call-start
  17.3 0.7 compare_select_fusion.1
  18.0 0.8 fusion.16
  18.8 12.2 %convert_reduce_fusion = f32[256,128]{1,0:T(8,128)S(1)} fusion(s32[256,128]{1,0:T(8,128)} %param.23, pred[256,128]{1,0:T(8,128)(4,1)S(1)} %fusion.16), kind=kLoop, calls=%fused_computation.5 | loop fusion | flops 20938752 | bytes 294912 | tf_op jit(solution)/shard_map/reduce_sum | solution.py:62
  31.0 1.4 scatter_custom_fusion.1
  32.5 0.7 broadcast_multiply_fusion
  33.1 1.0 fusion.15
  34.2 0.0 collective-permute-done
  34.2 237.9 %all-gather.9.cloned.1.call-done = bf16[16,256,128]{2,0,1:T(8,128)(2,1)} async-done(((bf16[16,2,128]{2,0,1:T(8,128)(2,1)}), bf16[16,256,128]{2,0,1:T(8,128)(2,1)}) %all-gather.9.cloned.1.call-update) | async-done | bytes 1048592 | tf_op jit(solution)/shard_map/all_gather | solution.py:42
  272.1 1.5 pad_maximum_fusion
  273.5 6.8 %copy.31 = bf16[16,336,128]{0,2,1:T(8,128)(2,1)} copy(bf16[16,336,128]{2,0,1:T(8,128)(2,1)S(1)} %pad_maximum_fusion) | data formatting | bytes 2752512 | tf_op jit(solution)/shard_map/reshape | solution.py:48
  280.4 115.7 %gather_fusion.2 = bf16[32768,16]{1,0:T(8,128)(2,1)} fusion(bf16[16,43008]{0,1:T(8,128)(2,1)} %bitcast.28, s32[32768]{0:T(1024)S(1)} %fusion.15), kind=kCustom, calls=%fused_computation.2 | custom fusion | bytes 2228224 | tf_op jit(solution)/shard_map/gather | solution.py:55
  396.0 7.0 %copy.29 = bf16[256,128,16]{1,2,0:T(8,128)(2,1)S(1)} copy(bf16[256,128,16]{2,1,0:T(8,128)(2,1)} %bitcast.29) | data formatting | bytes 2097152 | tf_op jit(solution)/shard_map/gather | solution.py:55
  403.1 21.0 %fusion.2 = f32[256,16,128]{2,1,0:T(8,128)S(1)} fusion(s32[256,128]{1,0:T(8,128)S(1)} %copy-done.1, pred[256,128]{1,0:T(8,128)(4,1)S(1)} %fusion.16, bf16[256,128,16]{1,2,0:T(8,128)(2,1)S(1)} %copy.29), kind=kOutput, calls=%fused_computation.9 | convolution fusion | flops 143130624 | bytes 3309568 | tf_op jit(solution)/shard_map/fte,teb->ftb/dot_general | solution.py:61
  424.1 0.0 copy-start.2
  424.1 8.9 %scatter_fusion = f32[16,64,128]{2,0,1:T(8,128)S(1)} fusion(f32[16,64,128]{2,0,1:T(8,128)S(1)} %broadcast_in_dim.24, s32[256]{0:T(256)S(1)} %compare_select_fusion.1, f32[256,16,128]{2,1,0:T(8,128)S(1)} %fusion.2), kind=kCustom, calls=%fused_computation.3 | custom fusion | flops 524288 | bytes 6292480 | tf_op jit(solution)/shard_map/scatter-add | solution.py:63
  433.0 0.8 copy_bitcast_fusion
  433.8 0.0 all-gather.7.cloned.1.call-update
  433.8 0.1 dynamic_slice.11
  433.9 2.0 fusion.20
  435.9 31.3 %all-gather.7.cloned.1.call-done = bf16[128,8192]{1,0:T(8,128)(2,1)} async-done(((bf16[16,8192]{1,0:T(8,128)(2,1)}), bf16[128,8192]{1,0:T(8,128)(2,1)}) %all-gather.7.cloned.1.call-update) | async-done | bytes 2097168 | tf_op jit(solution)/shard_map/all_gather | solution.py:71
  467.2 2.7 fusion.6
  (14 shorter events, 0.1 us)
Async XLA Ops:
  6.5 427.4 %copy-start = (bf16[128,128]{1,0:T(8,128)(2,1)S(1)}, bf16[128,128]{1,0:T(8,128)(2,1)}, u32[]{:S(2)}) copy-start(bf16[128,128]{1,0:T(8,128)(2,1)} %param.13) | copy-start | bytes 98308
  6.5 265.5 %all-gather.9.cloned.1.call-start = ((), (), s32[]{:S(2)}) async-start(), calls=%async_computation.2 | async-start | bytes 1056768 | tf_op jit(solution)/shard_map/all_gather | solution.py:42
  9.4 424.5 %all-gather.5.cloned.1.call-start = ((), (), s32[]{:S(2)}) async-start(), calls=%async_computation | async-start | bytes 2359296 | tf_op jit(solution)/shard_map/all_gather | solution.py:70
  10.7 23.5 %collective-permute-start = (bf16[16,8,128]{2,0,1:T(8,128)(2,1)S(1)}, bf16[16,8,128]{2,0,1:T(8,128)(2,1)S(1)}, u32[]{:S(2)}, u32[]{:S(2)}) collective-permute-start(bf16[16,8,128]{2,0,1:T(8,128)(2,1)S(1)} %get-tuple-element.5), channel_id=1, source_target_pairs={{0,8},{8,16},{16,24},{24,32},{32,40},{40,48},{48,56},{56,64},{64,7... | collective-permute-start | bytes 98312 | tf_op jit(solution)/shard_map/ppermute | solution.py:15
  14.4 19.7 %collective-permute-start.1 = (bf16[16,8,128]{2,0,1:T(8,128)(2,1)S(1)}, bf16[16,8,128]{2,0,1:T(8,128)(2,1)S(1)}, u32[]{:S(2)}, u32[]{:S(2)}) collective-permute-start(bf16[16,8,128]{2,0,1:T(8,128)(2,1)S(1)} %get-tuple-element.6), channel_id=1, source_target_pairs={{8,0},{16,8},{24,16},{32,24},{40,32},{48,40},{56,48},{64,56},{72,6... | collective-permute-start | bytes 98312 | tf_op jit(solution)/shard_map/ppermute | solution.py:18
  16.6 450.6 %all-gather.7.cloned.1.call-start = ((), (), s32[]{:S(2)}) async-start(), calls=%async_computation.1 | async-start | bytes 2359296 | tf_op jit(solution)/shard_map/all_gather | solution.py:71
  396.0 7.0 %copy-start.1 = (s32[256,128]{1,0:T(8,128)S(1)}, s32[256,128]{1,0:T(8,128)}, u32[]{:S(2)}) copy-start(s32[256,128]{1,0:T(8,128)} %param.23) | copy-start | bytes 393220
  424.1 9.7 %copy-start.2 = (f32[128]{0:T(128)S(1)}, f32[128]{0:T(128)}, u32[]{:S(2)}) copy-start(f32[128]{0:T(128)} %param.15) | copy-start | bytes 1540
Sparse Core Ops, SparseCore 0:
  11.4 260.5 all-gather.8
  274.8 33.2 all-gather.4
  433.9 33.1 all-gather.6
where the time goes:
time: 478 us; the launch traced here: 476 us
  waiting for transfers between devices  269 us (56%)
  local copies, waits for them, and re-layouts  132 us (28%)
  other arithmetic  29.3 us (6%)
  matrix products  25.6 us (5%)
  between operations  13.9 us (3%)
  starting transfers between devices  5.93 us (1%)
    all_gather x1, waiting for transfers between devices, shards(): hub_rows = lax.all_gather(hub_local, 'graph', axis=1, tiled=True)  238 us
    gather x2, local copies, waits for them, and re-layouts, shards(): gathered = flat_table[:, source]  123 us
    all_gather x1, waiting for transfers between devices, shards(): mean_piece = lax.all_gather(own_means, 'feat', axis=0, tiled=True)  31.3 us
    dot_general x1, matrix products, shards(): jnp.einsum('fte,teb->ftb', gathered, one_hot, preferred_element_type=jnp....  21 us
    reduce_sum x1, other arithmetic, shards(): tile_degree = jnp.sum(one_hot, axis=1, dtype=jnp.float32)  12.2 us
  transfers between devices with their start and end apart: 5, of which 2 were waited for; matrix products, arithmetic and copies ran while one was open for 38% of the time, Pallas kernels for 0%

commit v1 on v0

v1 whole, which is shorter than its diff:
```python
import jax
import jax.numpy as jnp
from jax import lax
from jax.experimental import pallas as pl
from jax.experimental.pallas import tpu as pltpu
from jax.sharding import PartitionSpec as P

BLOCK = 128
GROUP = 8
Z, X = 32, 4
STRIDE = 2


def pick_kernel(hub_pick, halo_send, features, hub_out, halo_out):
    def copy(out, picks):
        for i in range(out.shape[0]):
            start = pl.multiple_of(picks[i] * BLOCK, BLOCK)
            out[i] = features[:, pl.ds(start, BLOCK)]

    copy(hub_out, hub_pick)
    copy(halo_out, halo_send)


def pick_blocks(features, hub_pick, halo_send):
    rows = features.shape[0]
    smem = pl.BlockSpec(memory_space=pltpu.SMEM)
    vmem = pl.BlockSpec(memory_space=pltpu.VMEM)
    return pl.pallas_call(
        pick_kernel,
        out_shape=[
            jax.ShapeDtypeStruct((hub_pick.shape[0], rows, BLOCK), features.dtype),
            jax.ShapeDtypeStruct((halo_send.shape[0], rows, BLOCK), features.dtype),
        ],
        in_specs=[smem, smem, vmem],
        out_specs=[vmem, vmem],
        name="pick_blocks",
    )(hub_pick, halo_send, features)


def table_row(slot, own, hubs):
    hub = slot - own
    group = X * STRIDE
    owner = hub >> 1
    place = ((owner & (group - 1)) * (hubs // group)) + ((owner // group) << 1) + (hub & 1)
    return jnp.where((hub >= 0) & (hub < hubs), own + place, slot)


def mean_kernel(
    tile_dst,
    tile_src,
    tile_edges,
    tile_count,
    features,
    edge_src,
    edge_dst,
    hub_rows,
    halo_low,
    halo_high,
    mean_out,
    table,
    sums,
    sems,
):
    rows = features.shape[0]
    own = features.shape[1] // BLOCK
    hubs = hub_rows.shape[0]
    halo = halo_low.shape[0]
    copies = [
        pltpu.make_async_copy(hub_rows, table.at[pl.ds(own, hubs)], sems.at[0]),
        pltpu.make_async_copy(halo_low, table.at[pl.ds(own + hubs, halo)], sems.at[1]),
        pltpu.make_async_copy(halo_high, table.at[pl.ds(own + hubs + halo, halo)], sems.at[2]),
    ]
    for copy in copies:
        copy.start()
    for b in range(own):
        table[b] = features[:, b * BLOCK : (b + 1) * BLOCK]
        sums[b] = jnp.zeros(sums.shape[1:], jnp.float32)
    for copy in copies:
        copy.wait()

    count = tile_count[0]
    lane = lax.broadcasted_iota(jnp.int32, (8, BLOCK), 1)
    node = lax.broadcasted_iota(jnp.int32, (BLOCK, BLOCK), 0)
    ones = jnp.ones((sums.shape[1] - rows, BLOCK), jnp.float32)

    @pl.loop(0, (count + GROUP - 1) // GROUP)
    def _(step):
        first = pl.multiple_of(step * GROUP, GROUP)
        sources = edge_src[pl.ds(first, GROUP), :]
        targets = edge_dst[pl.ds(first, GROUP), :]
        parts = []
        for i in range(GROUP):
            tile = first + i
            live = jnp.where(tile < count, tile_edges[tile], 0)
            block = table[table_row(tile_src[tile], own, hubs)].astype(jnp.float32)
            index = jnp.broadcast_to(sources[i : i + 1], (8, BLOCK))
            values = [
                jnp.take_along_axis(block[r : r + 8], index, axis=1, mode="promise_in_bounds")
                for r in range(0, rows, 8)
            ]
            left = jnp.concatenate(values + [ones], axis=0).astype(jnp.bfloat16)
            target = jnp.where(lane < live, jnp.broadcast_to(targets[i : i + 1], (8, BLOCK)), -1)
            hits = node == jnp.broadcast_to(target[:1], (BLOCK, BLOCK))
            right = jnp.where(hits, 1.0, 0.0).astype(jnp.bfloat16)
            parts.append(
                lax.dot_general(
                    left, right, (((1,), (1,)), ((), ())), preferred_element_type=jnp.float32
                )
            )
        for i in range(GROUP):
            place = tile_dst[first + i]
            sums[place] = sums[place] + parts[i]

    per = own // mean_out.shape[0]
    for b in range(own):
        total = sums[b]
        degree = jnp.maximum(total[rows : rows + 8], 1.0)
        mean = jnp.concatenate([total[r : r + 8] / degree for r in range(0, rows, 8)], axis=0)
        at = (b % per) * BLOCK
        mean_out[b // per, :, at : at + BLOCK] = mean.astype(mean_out.dtype)


def neighbour_mean(
    features, hub_rows, halo_low, halo_high, tile_dst, tile_src, tile_edges, tile_count, edge_src, edge_dst, parts
):
    rows, nodes = features.shape
    own = nodes // BLOCK
    slots = own + hub_rows.shape[0] + 2 * halo_low.shape[0]
    smem = pl.BlockSpec(memory_space=pltpu.SMEM)
    vmem = pl.BlockSpec(memory_space=pltpu.VMEM)
    anywhere = pl.BlockSpec(memory_space=pl.ANY)
    return pl.pallas_call(
        mean_kernel,
        out_shape=jax.ShapeDtypeStruct((parts, rows, nodes // parts), features.dtype),
        in_specs=[smem] * 4 + [vmem] * 3 + [anywhere] * 3,
        out_specs=vmem,
        scratch_shapes=[
            pltpu.VMEM((slots, rows, BLOCK), features.dtype),
            pltpu.VMEM((own, 2 * rows, BLOCK), jnp.float32),
            pltpu.SemaphoreType.DMA((3,)),
        ],
        compiler_params=pltpu.CompilerParams(vmem_limit_bytes=32 * 1024 * 1024),
        name="neighbour_mean",
    )(tile_dst, tile_src, tile_edges, tile_count, features, edge_src, edge_dst, hub_rows, halo_low, halo_high)


def project_kernel(features, mean, w_self, w_neigh, bias, out):
    total = jnp.dot(w_self[...], features[...], preferred_element_type=jnp.float32) + jnp.dot(
        w_neigh[...], mean[...], preferred_element_type=jnp.float32
    )
    out[...] = jnp.maximum(total + bias[...], 0.0).astype(out.dtype)


def project(features, mean, w_self, w_neigh, bias):
    return pl.pallas_call(
        project_kernel,
        out_shape=jax.ShapeDtypeStruct(mean.shape, mean.dtype),
        name="project",
    )(features, mean, w_self, w_neigh, bias[:, None])


def shards(
    features,
    w_self,
    w_neigh,
    bias,
    hub_pick,
    halo_send,
    tile_dst,
    tile_src,
    tile_edges,
    tile_count,
    edge_src,
    edge_dst,
):
    rows, nodes = features.shape
    parts = lax.axis_size("feat")
    count = lax.axis_size("graph")
    halo = halo_send.shape[0] // 2
    hub_local, outgoing = pick_blocks(features, hub_pick, halo_send)

    along_z = [[X * z + x for z in range(r, Z, STRIDE)] for r in range(STRIDE) for x in range(X)]
    nearby = [
        [X * (z + r) + x for r in range(STRIDE) for x in range(X)] for z in range(0, Z, STRIDE)
    ]
    column = lax.all_gather(hub_local, "graph", axis_index_groups=along_z)
    spread = jnp.broadcast_to(column[None], (X * STRIDE, *column.shape))
    hub_rows = lax.all_to_all(spread, "graph", 0, 0, axis_index_groups=nearby)
    hub_rows = hub_rows.reshape(-1, rows, BLOCK)

    forward = [(i, (i + 1) % count) for i in range(count)]
    backward = [(target, source) for source, target in forward]
    halo_low = lax.ppermute(outgoing[halo:], "graph", forward)
    halo_high = lax.ppermute(outgoing[:halo], "graph", backward)

    means = neighbour_mean(
        features, hub_rows, halo_low, halo_high, tile_dst, tile_src, tile_edges, tile_count, edge_src, edge_dst, parts
    )
    every = lax.all_gather(features, "feat", axis=0, tiled=True)
    width = nodes // parts
    inputs = lax.dynamic_slice_in_dim(every, lax.axis_index("feat") * width, width, 1)
    means = lax.all_to_all(means, "feat", 0, 0).reshape(parts * rows, width)
    updated = project(inputs, means, w_self, w_neigh, bias).reshape(parts, rows, width)
    updated = lax.all_to_all(updated, "feat", 0, 0)
    return jnp.transpose(updated, (1, 0, 2)).reshape(rows, nodes)


def solution(mesh):
    in_specs = (
        P("feat", "graph"),
        P(),
        P(),
        P(),
        P("graph"),
        P("graph"),
        P("graph"),
        P("graph"),
        P("graph"),
        P("graph"),
        P("graph", None),
        P("graph", None),
    )
    out_specs = P("feat", "graph")
    return jax.shard_map(shards, mesh=mesh, in_specs=in_specs, out_specs=out_specs, check_vma=False)
```

time: 478 us -> 127 us (0.27)
  waiting for transfers between devices: 269 us -> 23 us
  local copies, waits for them, and re-layouts: 132 us -> 4.99 us
  blocking collectives: 0 us -> 59.3 us
  other arithmetic: 29.3 us -> 0 us
  matrix products: 25.6 us -> 0 us
  starting transfers between devices: 5.93 us -> 15.6 us
  Pallas kernels: 0 us -> 8.7 us
    all_gather x3 -> x1, waiting for transfers between devices: 269 us -> 17.5 us  [shards(): every = lax.all_gather(features, 'feat', axis=0, tiled=True)]
    gather x4 -> x0, local copies, waits for them, and re-layouts: 124 us -> none  [the longest x2 123 us: shards(): gathered = flat_table[:, source]]
    all_gather x0 -> x1, blocking collectives: none -> 47.8 us  [shards(): column = lax.all_gather(hub_local, 'graph', axis_index_groups=along_z)]
    dot_general x3 -> x0, matrix products: 25.6 us -> none  [the longest x1 21 us: shards(): jnp.einsum('fte,teb->ftb', gathered, one_hot, preferred_element_type=jnp....]
    reduce_sum x1 -> x0, other arithmetic: 12.2 us -> none  [shards(): tile_degree = jnp.sum(one_hot, axis=1, dtype=jnp.float32)]
    all_to_all x0 -> x1, blocking collectives: none -> 11.5 us  [shards(): updated = lax.all_to_all(updated, 'feat', 0, 0)]
    scatter-add x2 -> x0, other arithmetic: 10.4 us -> none  [the longest x1 8.92 us: shards(): jnp.zeros((feat_rows, block_count, BLOCK), jnp.float32).at[:, tile_dst, :]]
    all_to_all x0 -> x2, starting transfers between devices: none -> 9.76 us  [the longest x1 5.28 us: shards(): hub_rows = lax.all_to_all(spread, 'graph', 0, 0, axis_index_groups=nearby)]
  transfers between devices with their start and end apart: 5 -> 5, of which waited for: 2 -> 3; matrix products, arithmetic and copies ran while one was open for 38% -> 2% of each run, Pallas kernels for 0% -> 4%
where the time goes in v1:
time: 127 us; the launch traced here: 126 us
  blocking collectives  59.3 us (47%)
  waiting for transfers between devices  23 us (18%)
  starting transfers between devices  15.6 us (12%)
  between operations  14.1 us (11%)
  Pallas kernels  8.7 us (7%)
  local copies, waits for them, and re-layouts  4.99 us (4%)
    all_gather x1, blocking collectives, shards(): column = lax.all_gather(hub_local, 'graph', axis_index_groups=along_z)  47.8 us
    all_gather x1, waiting for transfers between devices, shards(): every = lax.all_gather(features, 'feat', axis=0, tiled=True)  17.5 us
    all_to_all x1, blocking collectives, shards(): updated = lax.all_to_all(updated, 'feat', 0, 0)  11.5 us
    all_to_all x1, starting transfers between devices, shards(): hub_rows = lax.all_to_all(spread, 'graph', 0, 0, axis_index_groups=nearby)  5.28 us
    pallas_call x1, Pallas kernels, neighbour_mean(): pl.pallas_call(mean_kernel, out_shape=jax.ShapeDtypeStruct((parts, rows,...  5 us
    all_to_all x1, starting transfers between devices, shards(): means = lax.all_to_all(means, 'feat', 0, 0).reshape(parts * rows, width)  4.48 us
    ppermute x1, waiting for transfers between devices, shards(): halo_high = lax.ppermute(outgoing[:halo], 'graph', backward)  3.42 us
    ppermute x1, starting transfers between devices, shards(): halo_low = lax.ppermute(outgoing[halo:], 'graph', forward)  3.37 us
  transfers between devices with their start and end apart: 5, of which 3 were waited for; matrix products, arithmetic and copies ran while one was open for 2% of the time, Pallas kernels for 4%

profile of v1, /device:TPU:6, one launch (start us, length us, event | category | flops | bytes accessed | tf_op | source)
XLA Modules:
  0.0 125.8 jit_solution(8789633142450185837)
XLA Ops:
  6.5 0.0 copy-start
  6.5 0.0 copy-start.3
  6.5 0.0 copy-start.2
  6.6 1.7 %pick_blocks.1 = (bf16[2,16,128]{2,1,0:T(8,128)(2,1)}, bf16[16,16,128]{2,1,0:T(8,128)(2,1)}) custom-call(s32[2]{0:T(128)} %hub_pick.1, s32[16]{0:T(128)} %halo_send.1, bf16[16,8192]{1,0:T(8,128)(2,1)} %features.3), custom_call_target="tpu_custom_call" | custom-call | tf_op jit(solution)/shard_map/pick_blocks/pallas_call | solution.py:28
  8.2 47.8 %all-gather = bf16[32,16,128]{2,1,0:T(8,128)(2,1)S(1)} all-gather(bf16[2,16,128]{2,1,0:T(8,128)(2,1)} %get-tuple-element.7), channel_id=2, replica_groups={{0,64,128,192,256,320,384,448,512,576,640,704,768,832,896,960},{8,72,13..., dimensions={0}, use_global_device_ids=true | all-gather | bytes 139264 | tf_op jit(solution)/shard_map/all_gather | solution.py:186
  56.1 1.1 broadcast_in_dim.4
  57.2 5.3 %all-to-all-start = ((bf16[8,16,2,16,128]{4,3,2,1,0:T(8,128)(2,1)}), bf16[8,16,2,16,128]{4,3,2,1,0:T(8,128)(2,1)S(1)}, u32[]{:S(2)}, u32[]{:S(2)}) async-start(bf16[8,16,2,16,128]{4,3,2,1,0:T(8,128)(2,1)} %broadcast_in_dim.4), calls=%async_computation | async-start | bytes 2097152 | tf_op jit(solution)/shard_map/all_to_all | solution.py:188
  62.5 0.0 all-gather.3.cloned.1.call-start
  62.5 0.7 all-gather.3.cloned.1.call-update
  63.2 0.0 copy-done.7
  63.3 3.4 %collective-permute-start = (bf16[8,16,128]{2,1,0:T(8,128)(2,1)S(1)}, bf16[8,16,128]{2,1,0:T(8,128)(2,1)S(1)}, u32[]{:S(2)}, u32[]{:S(2)}) collective-permute-start(bf16[8,16,128]{2,1,0:T(8,128)(2,1)S(1)} %get-tuple-element.10), channel_id=1, source_target_pairs={{0,8},{8,16},{16,24},{24,32},{32,40},{40,48},{48,56},{56,64},{64,7... | collective-permute-start | bytes 98312 | tf_op jit(solution)/shard_map/ppermute | solution.py:193
  66.6 2.5 %collective-permute-start.1 = (bf16[8,16,128]{2,1,0:T(8,128)(2,1)S(1)}, bf16[8,16,128]{2,1,0:T(8,128)(2,1)S(1)}, u32[]{:S(2)}, u32[]{:S(2)}) collective-permute-start(bf16[8,16,128]{2,1,0:T(8,128)(2,1)S(1)} %get-tuple-element.9), channel_id=1, source_target_pairs={{8,0},{16,8},{24,16},{32,24},{40,32},{48,40},{56,48},{64,56},{72,6... | collective-permute-start | bytes 98312 | tf_op jit(solution)/shard_map/ppermute | solution.py:194
  69.8 1.4 %collective-permute-done.halo_low = bf16[8,16,128]{2,1,0:T(8,128)(2,1)S(1)} collective-permute-done((bf16[8,16,128]{2,1,0:T(8,128)(2,1)S(1)}, bf16[8,16,128]{2,1,0:T(8,128)(2,1)S(1)}, u32[]{:S(2)}, u32[]{:S(2)}) %collective-permute-start) | collective-permute-done | bytes 32800 | tf_op jit(solution)/shard_map/ppermute | solution.py:193
  71.1 3.4 %collective-permute-done.1.halo_high = bf16[8,16,128]{2,1,0:T(8,128)(2,1)S(1)} collective-permute-done((bf16[8,16,128]{2,1,0:T(8,128)(2,1)S(1)}, bf16[8,16,128]{2,1,0:T(8,128)(2,1)S(1)}, u32[]{:S(2)}, u32[]{:S(2)}) %collective-permute-start.1) | collective-permute-done | bytes 32800 | tf_op jit(solution)/shard_map/ppermute | solution.py:194
  74.6 0.0 all-to-all-done
  74.6 0.0 copy-done
  74.6 0.0 copy-done.3
  74.6 0.0 copy-done.4
  74.6 0.0 copy-done.5
  74.6 0.0 copy-done.1
  74.6 0.0 copy-done.2
  74.6 5.0 %neighbour_mean.1 = bf16[8,16,1024]{2,1,0:T(8,128)(2,1)} custom-call(s32[256]{0:T(256)S(1)} %copy-done.3, s32[256]{0:T(256)S(1)} %copy-done.4, s32[256]{0:T(256)S(1)} %copy-done.5, s32[1]{0:T(128)S(6)} %copy.18.tile_count, bf16[16,8192]{1,0:T(8,128)(2,1)S(1)} %copy-done, s32[256,128]{1,0:T(8,128)S(1)} %copy-done.1, s32[256,128]{1,0:T(8,128)S(1)} %copy-done.2, ...), custom_call_target="tpu_custom_call" | custom-call | tf_op jit(solution)/shard_map/neighbour_mean/pallas_call | solution.py:132
  79.6 4.5 %all-to-all-start.1 = ((bf16[8,16,1024]{2,1,0:T(8,128)(2,1)}), bf16[8,16,1024]{2,1,0:T(8,128)(2,1)S(1)}, u32[]{:S(2)}, u32[]{:S(2)}) async-start(bf16[8,16,1024]{2,1,0:T(8,128)(2,1)} %neighbour_mean.1), calls=%async_computation.1 | async-start | bytes 524288 | tf_op jit(solution)/shard_map/all_to_all | solution.py:202
  84.1 0.0 copy-done.8
  84.1 0.7 copy.15.bias
  84.8 17.5 %all-gather.3.cloned.1.call-done = bf16[128,8192]{1,0:T(8,128)(2,1)} async-done(((bf16[16,8192]{1,0:T(8,128)(2,1)}), bf16[128,8192]{1,0:T(8,128)(2,1)}) %all-gather.3.cloned.1.call-update) | async-done | bytes 2097168 | tf_op jit(solution)/shard_map/all_gather | solution.py:199
  102.3 1.7 %constant_dynamic-slice_fusion.features = bf16[128,1024]{1,0:T(8,128)(2,1)} fusion(bf16[128,8192]{1,0:T(8,128)(2,1)} %all-gather.3.cloned.1.call-done, s32[]{:T(128)S(6)} %select_n.3), kind=kLoop, calls=%fused_computation | loop fusion | bytes 524292 | tf_op jit(solution)/shard_map/dynamic_slice | solution.py:201
  104.0 0.0 all-to-all-done.1
  104.0 0.7 copy-done.6
  104.7 2.0 %project.1 = bf16[128,1024]{1,0:T(8,128)(2,1)} custom-call(bf16[128,1024]{1,0:T(8,128)(2,1)} %constant_dynamic-slice_fusion.features, bf16[128,1024]{1,0:T(8,128)(2,1)} %bitcast.9, bf16[128,128]{1,0:T(8,128)(2,1)} %w_self.1, bf16[128,128]{1,0:T(8,128)(2,1)} %w_neigh.1, f32[128,1]{1,0:T(8,128)} %copy.15.bias), custom_call_target="tpu_custom_call" | custom-call | tf_op jit(solution)/shard_map/project/pallas_call | solution.py:155
  106.7 11.5 %all_to_all.15 = bf16[8,16,1024]{2,1,0:T(8,128)(2,1)S(1)} all-to-all(bf16[8,16,1024]{2,1,0:T(8,128)(2,1)} %bitcast.10), channel_id=1, replica_groups=mesh['graph'=128,'feat'=8] {'feat'}, dimensions={0} | all-to-all | bytes 524288 | tf_op jit(solution)/shard_map/all_to_all | solution.py:204
  118.2 0.7 copy.17
  (7 shorter events, 0.0 us)
Async XLA Ops:
  6.5 68.0 %copy-start = (bf16[16,8192]{1,0:T(8,128)(2,1)S(1)}, bf16[16,8192]{1,0:T(8,128)(2,1)}, u32[]{:S(2)}) copy-start(bf16[16,8192]{1,0:T(8,128)(2,1)} %features.3) | copy-start | bytes 786436
  6.5 68.0 %copy-start.3 = (s32[256]{0:T(256)S(1)}, s32[256]{0:T(256)}, u32[]{:S(2)}) copy-start(s32[256]{0:T(256)} %tile_dst.1) | copy-start | bytes 3076
  6.5 68.0 %copy-start.4 = (s32[256]{0:T(256)S(1)}, s32[256]{0:T(256)}, u32[]{:S(2)}) copy-start(s32[256]{0:T(256)} %tile_src.1) | copy-start | bytes 3076
  6.5 68.0 %copy-start.5 = (s32[256]{0:T(256)S(1)}, s32[256]{0:T(256)}, u32[]{:S(2)}) copy-start(s32[256]{0:T(256)} %tile_edges.1) | copy-start | bytes 3076
  6.5 68.0 %copy-start.1 = (s32[256,128]{1,0:T(8,128)S(1)}, s32[256,128]{1,0:T(8,128)}, u32[]{:S(2)}) copy-start(s32[256,128]{1,0:T(8,128)} %edge_src.1) | copy-start | bytes 393220
  6.5 68.1 %copy-start.2 = (s32[256,128]{1,0:T(8,128)S(1)}, s32[256,128]{1,0:T(8,128)}, u32[]{:S(2)}) copy-start(s32[256,128]{1,0:T(8,128)} %edge_dst.1) | copy-start | bytes 393220
  8.2 55.0 %copy-start.7 = (bf16[16,16,128]{2,1,0:T(8,128)(2,1)S(1)}, bf16[16,16,128]{2,1,0:T(8,128)(2,1)}, u32[]{:S(2)}) copy-start(bf16[16,16,128]{2,1,0:T(8,128)(2,1)} %get-tuple-element.8) | copy-start | bytes 196612
  57.2 26.9 %copy-start.8 = (f32[128]{0:T(128)S(1)}, f32[128]{0:T(128)}, u32[]{:S(2)}) copy-start(f32[128]{0:T(128)} %param.15) | copy-start | bytes 1540
  57.2 17.3 %all-to-all-start = ((bf16[8,16,2,16,128]{4,3,2,1,0:T(8,128)(2,1)}), bf16[8,16,2,16,128]{4,3,2,1,0:T(8,128)(2,1)S(1)}, u32[]{:S(2)}, u32[]{:S(2)}) async-start(bf16[8,16,2,16,128]{4,3,2,1,0:T(8,128)(2,1)} %broadcast_in_dim.4), calls=%async_computation | async-start | bytes 2097152 | tf_op jit(solution)/shard_map/all_to_all | solution.py:188
  62.5 39.8 %all-gather.3.cloned.1.call-start = ((), (), s32[]{:S(2)}) async-start(), calls=%async_computation.3 | async-start | bytes 2359296 | tf_op jit(solution)/shard_map/all_gather | solution.py:199
  63.3 7.9 %collective-permute-start = (bf16[8,16,128]{2,1,0:T(8,128)(2,1)S(1)}, bf16[8,16,128]{2,1,0:T(8,128)(2,1)S(1)}, u32[]{:S(2)}, u32[]{:S(2)}) collective-permute-start(bf16[8,16,128]{2,1,0:T(8,128)(2,1)S(1)} %get-tuple-element.10), channel_id=1, source_target_pairs={{0,8},{8,16},{16,24},{24,32},{32,40},{40,48},{48,56},{56,64},{64,7... | collective-permute-start | bytes 98312 | tf_op jit(solution)/shard_map/ppermute | solution.py:193
  66.6 7.9 %collective-permute-start.1 = (bf16[8,16,128]{2,1,0:T(8,128)(2,1)S(1)}, bf16[8,16,128]{2,1,0:T(8,128)(2,1)S(1)}, u32[]{:S(2)}, u32[]{:S(2)}) collective-permute-start(bf16[8,16,128]{2,1,0:T(8,128)(2,1)S(1)} %get-tuple-element.9), channel_id=1, source_target_pairs={{8,0},{16,8},{24,16},{32,24},{40,32},{48,40},{56,48},{64,56},{72,6... | collective-permute-start | bytes 98312 | tf_op jit(solution)/shard_map/ppermute | solution.py:194
  79.6 24.4 %all-to-all-start.1 = ((bf16[8,16,1024]{2,1,0:T(8,128)(2,1)}), bf16[8,16,1024]{2,1,0:T(8,128)(2,1)S(1)}, u32[]{:S(2)}, u32[]{:S(2)}) async-start(bf16[8,16,1024]{2,1,0:T(8,128)(2,1)} %neighbour_mean.1), calls=%async_computation.1 | async-start | bytes 524288 | tf_op jit(solution)/shard_map/all_to_all | solution.py:202
  104.0 0.7 copy-start.6
Sparse Core Ops, SparseCore 0:
  66.1 36.2 all-gather.2

commit v2 on v1

--- a/solution.py
+++ b/solution.py
@@ -56,7 +56,7 @@
     hub_rows,
     halo_low,
     halo_high,
-    mean_out,
+    shares,
     table,
     sums,
     sems,
@@ -111,13 +111,14 @@
             place = tile_dst[first + i]
             sums[place] = sums[place] + parts[i]
 
-    per = own // mean_out.shape[0]
+    per = own // shares.shape[0]
     for b in range(own):
         total = sums[b]
         degree = jnp.maximum(total[rows : rows + 8], 1.0)
         mean = jnp.concatenate([total[r : r + 8] / degree for r in range(0, rows, 8)], axis=0)
         at = (b % per) * BLOCK
-        mean_out[b // per, :, at : at + BLOCK] = mean.astype(mean_out.dtype)
+        shares[b // per, :rows, at : at + BLOCK] = table[b]
+        shares[b // per, rows:, at : at + BLOCK] = mean.astype(shares.dtype)
 
 
 def neighbour_mean(
@@ -131,7 +132,7 @@
     anywhere = pl.BlockSpec(memory_space=pl.ANY)
     return pl.pallas_call(
         mean_kernel,
-        out_shape=jax.ShapeDtypeStruct((parts, rows, nodes // parts), features.dtype),
+        out_shape=jax.ShapeDtypeStruct((parts, 2 * rows, nodes // parts), features.dtype),
         in_specs=[smem] * 4 + [vmem] * 3 + [anywhere] * 3,
         out_specs=vmem,
         scratch_shapes=[
@@ -144,19 +145,27 @@
     )(tile_dst, tile_src, tile_edges, tile_count, features, edge_src, edge_dst, hub_rows, halo_low, halo_high)
 
 
-def project_kernel(features, mean, w_self, w_neigh, bias, out):
-    total = jnp.dot(w_self[...], features[...], preferred_element_type=jnp.float32) + jnp.dot(
-        w_neigh[...], mean[...], preferred_element_type=jnp.float32
+def project_kernel(shares, w_self, w_neigh, bias, out):
+    parts, rows, _ = out.shape
+
+    def whole(first):
+        return jnp.concatenate([shares[p, first : first + rows] for p in range(parts)], axis=0)
+
+    total = jnp.dot(w_self[...], whole(0), preferred_element_type=jnp.float32) + jnp.dot(
+        w_neigh[...], whole(rows), preferred_element_type=jnp.float32
     )
-    out[...] = jnp.maximum(total + bias[...], 0.0).astype(out.dtype)
-
-
-def project(features, mean, w_self, w_neigh, bias):
+    updated = jnp.maximum(total + bias[...], 0.0).astype(out.dtype)
+    for p in range(parts):
+        out[p] = updated[p * rows : (p + 1) * rows]
+
+
+def project(shares, w_self, w_neigh, bias):
+    parts, rows, width = shares.shape
     return pl.pallas_call(
         project_kernel,
-        out_shape=jax.ShapeDtypeStruct(mean.shape, mean.dtype),
+        out_shape=jax.ShapeDtypeStruct((parts, rows // 2, width), shares.dtype),
         name="project",
-    )(features, mean, w_self, w_neigh, bias[:, None])
+    )(shares, w_self, w_neigh, bias[:, None])
 
 
 def shards(
@@ -193,15 +202,11 @@
     halo_low = lax.ppermute(outgoing[halo:], "graph", forward)
     halo_high = lax.ppermute(outgoing[:halo], "graph", backward)
 
-    means = neighbour_mean(
+    shares = neighbour_mean(
         features, hub_rows, halo_low, halo_high, tile_dst, tile_src, tile_edges, tile_count, edge_src, edge_dst, parts
     )
-    every = lax.all_gather(features, "feat", axis=0, tiled=True)
-    width = nodes // parts
-    inputs = lax.dynamic_slice_in_dim(every, lax.axis_index("feat") * width, width, 1)
-    means = lax.all_to_all(means, "feat", 0, 0).reshape(parts * rows, width)
-    updated = project(inputs, means, w_self, w_neigh, bias).reshape(parts, rows, width)
-    updated = lax.all_to_all(updated, "feat", 0, 0)
+    shares = lax.all_to_all(shares, "feat", 0, 0)
+    updated = lax.all_to_all(project(shares, w_self, w_neigh, bias), "feat", 0, 0)
     return jnp.transpose(updated, (1, 0, 2)).reshape(rows, nodes)
 
 

time: 127 us -> 107 us (0.84)
  between operations: 14.1 us -> 0.76 us
  waiting for transfers between devices: 23 us -> 13.7 us
  Pallas kernels: 8.7 us -> 13.4 us
    all_gather x1 -> x0, waiting for transfers between devices: 17.5 us -> none  [shards(): every = lax.all_gather(features, 'feat', axis=0, tiled=True)]
    all_to_all x1, waiting for transfers between devices: 0.01 us -> 8.95 us  [shards(): shares = lax.all_to_all(shares, 'feat', 0, 0)]
    pallas_call x2, Pallas kernels: 7.03 us -> 11.7 us  [the longest x1 9.69 us: neighbour_mean(): pl.pallas_call(mean_kernel, out_shape=jax.ShapeDtypeStruct((parts, 2 * ro...]
    dynamic_slice x1 -> x0, local copies, waits for them, and re-layouts: 1.67 us -> none  [shards(): lax.dynamic_slice_in_dim(every, lax.axis_index('feat') * width, width, 1)]
  transfers between devices with their start and end apart: 5 -> 4, of which waited for: 3 -> 3; matrix products, arithmetic and copies ran while one was open for 2% -> 1% of each run, Pallas kernels for 4% -> 0%
where the time goes in v2:
time: 107 us; the launch traced here: 106 us
  blocking collectives  58.6 us (55%)
  starting transfers between devices  15.7 us (15%)
  waiting for transfers between devices  13.7 us (13%)
  Pallas kernels  13.4 us (13%)
  local copies, waits for them, and re-layouts  4.1 us (4%)
    all_gather x1, blocking collectives, shards(): column = lax.all_gather(hub_local, 'graph', axis_index_groups=along_z)  47.7 us
    all_to_all x1, blocking collectives, shards(): lax.all_to_all(project(shares, w_self, w_neigh, bias), 'feat', 0, 0)  10.8 us
    pallas_call x1, Pallas kernels, neighbour_mean(): pl.pallas_call(mean_kernel, out_shape=jax.ShapeDtypeStruct((parts, 2 * ro...  9.69 us
    all_to_all x1, waiting for transfers between devices, shards(): shares = lax.all_to_all(shares, 'feat', 0, 0)  8.95 us
    all_to_all x1, starting transfers between devices, shards(): hub_rows = lax.all_to_all(spread, 'graph', 0, 0, axis_index_groups=nearby)  5.28 us
    all_to_all x1, starting transfers between devices, shards(): shares = lax.all_to_all(shares, 'feat', 0, 0)  4.48 us
    ppermute x1, starting transfers between devices, shards(): halo_low = lax.ppermute(outgoing[halo:], 'graph', forward)  3.5 us
    ppermute x1, waiting for transfers between devices, shards(): halo_high = lax.ppermute(outgoing[:halo], 'graph', backward)  2.83 us
  transfers between devices with their start and end apart: 4, of which 3 were waited for; matrix products, arithmetic and copies ran while one was open for 1% of the time, Pallas kernels for 0%

profile of v2, /device:TPU:6, one launch (start us, length us, event | category | flops | bytes accessed | tf_op | source)
XLA Modules:
  0.0 106.2 jit_solution(5668173910890291833)
XLA Ops:
  0.0 1.6 %pick_blocks.1 = (bf16[2,16,128]{2,1,0:T(8,128)(2,1)}, bf16[16,16,128]{2,1,0:T(8,128)(2,1)}) custom-call(s32[2]{0:T(128)} %hub_pick.1, s32[16]{0:T(128)} %halo_send.1, bf16[16,8192]{1,0:T(8,128)(2,1)} %features.3), custom_call_target="tpu_custom_call" | custom-call | tf_op jit(solution)/shard_map/pick_blocks/pallas_call | solution.py:28
  1.6 47.7 %all-gather = bf16[32,16,128]{2,1,0:T(8,128)(2,1)S(1)} all-gather(bf16[2,16,128]{2,1,0:T(8,128)(2,1)} %get-tuple-element.7), channel_id=2, replica_groups={{0,64,128,192,256,320,384,448,512,576,640,704,768,832,896,960},{8,72,13..., dimensions={0}, use_global_device_ids=true | all-gather | bytes 139264 | tf_op jit(solution)/shard_map/all_gather | solution.py:195
  49.3 1.2 %broadcast_in_dim.4 = bf16[8,16,2,16,128]{4,3,2,1,0:T(8,128)(2,1)} broadcast(bf16[16,2,16,128]{3,2,1,0:T(8,128)(2,1)S(1)} %bitcast.8), dimensions={1,2,3,4} | broadcast | bytes 1179648 | tf_op jit(solution)/shard_map/broadcast_in_dim | solution.py:196
  50.5 0.0 copy-start.7
  50.5 0.0 copy-start
  50.5 0.0 copy-start.2
  50.5 5.3 %all-to-all-start = ((bf16[8,16,2,16,128]{4,3,2,1,0:T(8,128)(2,1)}), bf16[8,16,2,16,128]{4,3,2,1,0:T(8,128)(2,1)S(1)}, u32[]{:S(2)}, u32[]{:S(2)}) async-start(bf16[8,16,2,16,128]{4,3,2,1,0:T(8,128)(2,1)} %broadcast_in_dim.4), calls=%async_computation | async-start | bytes 2097152 | tf_op jit(solution)/shard_map/all_to_all | solution.py:197
  55.8 0.0 copy-start.1
  55.8 0.0 copy-done.7
  55.8 3.5 %collective-permute-start = (bf16[8,16,128]{2,1,0:T(8,128)(2,1)S(1)}, bf16[8,16,128]{2,1,0:T(8,128)(2,1)S(1)}, u32[]{:S(2)}, u32[]{:S(2)}) collective-permute-start(bf16[8,16,128]{2,1,0:T(8,128)(2,1)S(1)} %get-tuple-element.10), channel_id=1, source_target_pairs={{0,8},{8,16},{16,24},{24,32},{32,40},{40,48},{48,56},{56,64},{64,7... | collective-permute-start | bytes 98312 | tf_op jit(solution)/shard_map/ppermute | solution.py:202
  59.3 2.5 %collective-permute-start.1 = (bf16[8,16,128]{2,1,0:T(8,128)(2,1)S(1)}, bf16[8,16,128]{2,1,0:T(8,128)(2,1)S(1)}, u32[]{:S(2)}, u32[]{:S(2)}) collective-permute-start(bf16[8,16,128]{2,1,0:T(8,128)(2,1)S(1)} %get-tuple-element.9), channel_id=1, source_target_pairs={{8,0},{16,8},{24,16},{32,24},{40,32},{48,40},{56,48},{64,56},{72,6... | collective-permute-start | bytes 98312 | tf_op jit(solution)/shard_map/ppermute | solution.py:203
  61.8 0.0 copy-start.4
  61.8 0.0 copy-start.5
  62.5 0.0 copy-start.3
  62.5 1.9 %collective-permute-done.halo_low = bf16[8,16,128]{2,1,0:T(8,128)(2,1)S(1)} collective-permute-done((bf16[8,16,128]{2,1,0:T(8,128)(2,1)S(1)}, bf16[8,16,128]{2,1,0:T(8,128)(2,1)S(1)}, u32[]{:S(2)}, u32[]{:S(2)}) %collective-permute-start) | collective-permute-done | bytes 32800 | tf_op jit(solution)/shard_map/ppermute | solution.py:202
  64.4 2.8 %collective-permute-done.1.halo_high = bf16[8,16,128]{2,1,0:T(8,128)(2,1)S(1)} collective-permute-done((bf16[8,16,128]{2,1,0:T(8,128)(2,1)S(1)}, bf16[8,16,128]{2,1,0:T(8,128)(2,1)S(1)}, u32[]{:S(2)}, u32[]{:S(2)}) %collective-permute-start.1) | collective-permute-done | bytes 32800 | tf_op jit(solution)/shard_map/ppermute | solution.py:203
  67.2 0.0 all-to-all-done
  67.2 0.0 copy-done
  67.2 0.0 copy-done.2
  67.2 0.0 copy-done.1
  67.2 0.0 copy-done.4
  67.3 0.0 copy-done.5
  67.3 0.0 copy-done.3
  67.3 9.7 %neighbour_mean.1 = bf16[8,32,1024]{2,1,0:T(8,128)(2,1)} custom-call(s32[256]{0:T(256)S(1)} %copy-done.3, s32[256]{0:T(256)S(1)} %copy-done.4, s32[256]{0:T(256)S(1)} %copy-done.5, s32[1]{0:T(128)S(6)} %copy.19.tile_count, bf16[16,8192]{1,0:T(8,128)(2,1)S(1)} %copy-done, s32[256,128]{1,0:T(8,128)S(1)} %copy-done.1, s32[256,128]{1,0:T(8,128)S(1)} %copy-done.2, ...), custom_call_target="tpu_custom_call" | custom-call | tf_op jit(solution)/shard_map/neighbour_mean/pallas_call | solution.py:133
  77.0 4.5 %all-to-all-start.1 = ((bf16[8,32,1024]{2,1,0:T(8,128)(2,1)}), bf16[8,32,1024]{2,1,0:T(8,128)(2,1)S(1)}, u32[]{:S(2)}, u32[]{:S(2)}) async-start(bf16[8,32,1024]{2,1,0:T(8,128)(2,1)} %neighbour_mean.1), calls=%async_computation.1 | async-start | bytes 1048576 | tf_op jit(solution)/shard_map/all_to_all | solution.py:208
  81.5 0.7 copy-done.8
  82.1 0.7 copy.16.bias
  82.8 9.0 %all-to-all-done.1.shares = bf16[8,32,1024]{2,1,0:T(8,128)(2,1)S(1)} async-done(((bf16[8,32,1024]{2,1,0:T(8,128)(2,1)}), bf16[8,32,1024]{2,1,0:T(8,128)(2,1)S(1)}, u32[]{:S(2)}, u32[]{:S(2)}) %all-to-all-start.1) | async-done | bytes 524320 | tf_op jit(solution)/shard_map/all_to_all | solution.py:208
  91.8 0.8 copy-done.6
  92.6 2.1 %project.1 = bf16[8,16,1024]{2,1,0:T(8,128)(2,1)} custom-call(bf16[8,32,1024]{2,1,0:T(8,128)(2,1)} %copy-done.6, bf16[128,128]{1,0:T(8,128)(2,1)} %w_self.1, bf16[128,128]{1,0:T(8,128)(2,1)} %w_neigh.1, f32[128,1]{1,0:T(8,128)} %copy.16.bias), custom_call_target="tpu_custom_call" | custom-call | tf_op jit(solution)/shard_map/project/pallas_call | solution.py:164
  94.7 10.8 %all_to_all.15 = bf16[8,16,1024]{2,1,0:T(8,128)(2,1)S(1)} all-to-all(bf16[8,16,1024]{2,1,0:T(8,128)(2,1)} %project.1), channel_id=1, replica_groups=mesh['graph'=128,'feat'=8] {'feat'}, dimensions={0} | all-to-all | bytes 524288 | tf_op jit(solution)/shard_map/all_to_all | solution.py:209
  105.5 0.7 copy.18
  (3 shorter events, 0.0 us)
Async XLA Ops:
  50.5 5.3 %copy-start.7 = (bf16[16,16,128]{2,1,0:T(8,128)(2,1)S(1)}, bf16[16,16,128]{2,1,0:T(8,128)(2,1)}, u32[]{:S(2)}) copy-start(bf16[16,16,128]{2,1,0:T(8,128)(2,1)} %get-tuple-element.8) | copy-start | bytes 196612
  50.5 16.7 %copy-start = (bf16[16,8192]{1,0:T(8,128)(2,1)S(1)}, bf16[16,8192]{1,0:T(8,128)(2,1)}, u32[]{:S(2)}) copy-start(bf16[16,8192]{1,0:T(8,128)(2,1)} %features.3) | copy-start | bytes 786436
  50.5 16.7 %copy-start.2 = (s32[256,128]{1,0:T(8,128)S(1)}, s32[256,128]{1,0:T(8,128)}, u32[]{:S(2)}) copy-start(s32[256,128]{1,0:T(8,128)} %edge_dst.1) | copy-start | bytes 393220
  50.5 16.7 %all-to-all-start = ((bf16[8,16,2,16,128]{4,3,2,1,0:T(8,128)(2,1)}), bf16[8,16,2,16,128]{4,3,2,1,0:T(8,128)(2,1)S(1)}, u32[]{:S(2)}, u32[]{:S(2)}) async-start(bf16[8,16,2,16,128]{4,3,2,1,0:T(8,128)(2,1)} %broadcast_in_dim.4), calls=%async_computation | async-start | bytes 2097152 | tf_op jit(solution)/shard_map/all_to_all | solution.py:197
  55.8 11.5 %copy-start.1 = (s32[256,128]{1,0:T(8,128)S(1)}, s32[256,128]{1,0:T(8,128)}, u32[]{:S(2)}) copy-start(s32[256,128]{1,0:T(8,128)} %edge_src.1) | copy-start | bytes 393220
  55.8 8.6 %collective-permute-start = (bf16[8,16,128]{2,1,0:T(8,128)(2,1)S(1)}, bf16[8,16,128]{2,1,0:T(8,128)(2,1)S(1)}, u32[]{:S(2)}, u32[]{:S(2)}) collective-permute-start(bf16[8,16,128]{2,1,0:T(8,128)(2,1)S(1)} %get-tuple-element.10), channel_id=1, source_target_pairs={{0,8},{8,16},{16,24},{24,32},{32,40},{40,48},{48,56},{56,64},{64,7... | collective-permute-start | bytes 98312 | tf_op jit(solution)/shard_map/ppermute | solution.py:202
  59.3 7.9 %collective-permute-start.1 = (bf16[8,16,128]{2,1,0:T(8,128)(2,1)S(1)}, bf16[8,16,128]{2,1,0:T(8,128)(2,1)S(1)}, u32[]{:S(2)}, u32[]{:S(2)}) collective-permute-start(bf16[8,16,128]{2,1,0:T(8,128)(2,1)S(1)} %get-tuple-element.9), channel_id=1, source_target_pairs={{8,0},{16,8},{24,16},{32,24},{40,32},{48,40},{56,48},{64,56},{72,6... | collective-permute-start | bytes 98312 | tf_op jit(solution)/shard_map/ppermute | solution.py:203
  61.8 5.5 %copy-start.4 = (s32[256]{0:T(256)S(1)}, s32[256]{0:T(256)}, u32[]{:S(2)}) copy-start(s32[256]{0:T(256)} %tile_src.1) | copy-start | bytes 3076
  61.8 5.5 %copy-start.5 = (s32[256]{0:T(256)S(1)}, s32[256]{0:T(256)}, u32[]{:S(2)}) copy-start(s32[256]{0:T(256)} %tile_edges.1) | copy-start | bytes 3076
  62.5 4.8 %copy-start.3 = (s32[256]{0:T(256)S(1)}, s32[256]{0:T(256)}, u32[]{:S(2)}) copy-start(s32[256]{0:T(256)} %tile_dst.1) | copy-start | bytes 3076
  77.0 14.8 %all-to-all-start.1 = ((bf16[8,32,1024]{2,1,0:T(8,128)(2,1)}), bf16[8,32,1024]{2,1,0:T(8,128)(2,1)S(1)}, u32[]{:S(2)}, u32[]{:S(2)}) async-start(bf16[8,32,1024]{2,1,0:T(8,128)(2,1)} %neighbour_mean.1), calls=%async_computation.1 | async-start | bytes 1048576 | tf_op jit(solution)/shard_map/all_to_all | solution.py:208
  81.5 0.7 copy-start.8
  91.8 0.8 copy-start.6

commit v3 on v2

--- a/solution.py
+++ b/solution.py
@@ -6,7 +6,7 @@
 from jax.sharding import PartitionSpec as P
 
 BLOCK = 128
-GROUP = 8
+GROUP = 32
 Z, X = 32, 4
 STRIDE = 2
 
@@ -37,12 +37,10 @@
     )(hub_pick, halo_send, features)
 
 
-def table_row(slot, own, hubs):
-    hub = slot - own
+def hub_row(hub, hubs):
     group = X * STRIDE
     owner = hub >> 1
-    place = ((owner & (group - 1)) * (hubs // group)) + ((owner // group) << 1) + (hub & 1)
-    return jnp.where((hub >= 0) & (hub < hubs), own + place, slot)
+    return (owner & (group - 1)) * (hubs // group) + ((owner // group) << 1) + (hub & 1)
 
 
 def mean_kernel(
@@ -59,54 +57,64 @@
     shares,
     table,
     sums,
-    sems,
 ):
     rows = features.shape[0]
     own = features.shape[1] // BLOCK
     hubs = hub_rows.shape[0]
     halo = halo_low.shape[0]
-    copies = [
-        pltpu.make_async_copy(hub_rows, table.at[pl.ds(own, hubs)], sems.at[0]),
-        pltpu.make_async_copy(halo_low, table.at[pl.ds(own + hubs, halo)], sems.at[1]),
-        pltpu.make_async_copy(halo_high, table.at[pl.ds(own + hubs + halo, halo)], sems.at[2]),
-    ]
-    for copy in copies:
-        copy.start()
     for b in range(own):
         table[b] = features[:, b * BLOCK : (b + 1) * BLOCK]
         sums[b] = jnp.zeros(sums.shape[1:], jnp.float32)
-    for copy in copies:
-        copy.wait()
+    for b in range(halo):
+        table[own + b] = halo_low[b]
+        table[own + halo + b] = halo_high[b]
 
     count = tile_count[0]
     lane = lax.broadcasted_iota(jnp.int32, (8, BLOCK), 1)
-    node = lax.broadcasted_iota(jnp.int32, (BLOCK, BLOCK), 0)
-    ones = jnp.ones((sums.shape[1] - rows, BLOCK), jnp.float32)
+    node = lax.broadcasted_iota(jnp.int32, (BLOCK, BLOCK), 0).astype(jnp.bfloat16)
+    one, zero = jnp.ones((), jnp.bfloat16), jnp.zeros((), jnp.bfloat16)
+    ones = jnp.ones((rows, BLOCK), jnp.bfloat16)
+    blank = jnp.zeros((2 * rows, BLOCK), jnp.bfloat16)
 
     @pl.loop(0, (count + GROUP - 1) // GROUP)
     def _(step):
         first = pl.multiple_of(step * GROUP, GROUP)
         sources = edge_src[pl.ds(first, GROUP), :]
         targets = edge_dst[pl.ds(first, GROUP), :]
-        parts = []
+        lefts, rights, parts = [], [], []
         for i in range(GROUP):
             tile = first + i
-            live = jnp.where(tile < count, tile_edges[tile], 0)
-            block = table[table_row(tile_src[tile], own, hubs)].astype(jnp.float32)
+            slot = tile_src[tile]
+            hub = slot - own
+            is_hub = (hub >= 0) & (hub < hubs)
+            near = table[jnp.where(is_hub, 0, jnp.where(hub < 0, slot, slot - hubs))]
+            far = hub_rows[jnp.where(is_hub, hub_row(hub, hubs), 0)]
+            block = jnp.where(is_hub, far, near).astype(jnp.float32)
             index = jnp.broadcast_to(sources[i : i + 1], (8, BLOCK))
             values = [
                 jnp.take_along_axis(block[r : r + 8], index, axis=1, mode="promise_in_bounds")
                 for r in range(0, rows, 8)
             ]
-            left = jnp.concatenate(values + [ones], axis=0).astype(jnp.bfloat16)
+            values = jnp.concatenate(values, axis=0).astype(jnp.bfloat16)
+            lefts.append(jnp.concatenate([values, ones], axis=0))
+            live = jnp.where(tile < count, tile_edges[tile], 0)
             target = jnp.where(lane < live, jnp.broadcast_to(targets[i : i + 1], (8, BLOCK)), -1)
-            hits = node == jnp.broadcast_to(target[:1], (BLOCK, BLOCK))
-            right = jnp.where(hits, 1.0, 0.0).astype(jnp.bfloat16)
-            parts.append(
-                lax.dot_general(
-                    left, right, (((1,), (1,)), ((), ())), preferred_element_type=jnp.float32
-                )
+            hits = node == jnp.broadcast_to(target[:1].astype(jnp.bfloat16), (BLOCK, BLOCK))
+            rights.append(jnp.where(hits, one, zero))
+        for i in range(0, GROUP, 2):
+            left = jnp.concatenate(
+                [
+                    jnp.concatenate([lefts[i], blank], axis=1),
+                    jnp.concatenate([blank, lefts[i + 1]], axis=1),
+                ],
+                axis=0,
             )
+            right = jnp.concatenate([rights[i], rights[i + 1]], axis=1)
+            both = lax.dot_general(
+                left, right, (((1,), (1,)), ((), ())), preferred_element_type=jnp.float32
+            )
+            parts.append(both[: rows + 8])
+            parts.append(both[2 * rows : 3 * rows + 8])
         for i in range(GROUP):
             place = tile_dst[first + i]
             sums[place] = sums[place] + parts[i]
@@ -126,19 +134,16 @@
 ):
     rows, nodes = features.shape
     own = nodes // BLOCK
-    slots = own + hub_rows.shape[0] + 2 * halo_low.shape[0]
     smem = pl.BlockSpec(memory_space=pltpu.SMEM)
     vmem = pl.BlockSpec(memory_space=pltpu.VMEM)
-    anywhere = pl.BlockSpec(memory_space=pl.ANY)
     return pl.pallas_call(
         mean_kernel,
         out_shape=jax.ShapeDtypeStruct((parts, 2 * rows, nodes // parts), features.dtype),
-        in_specs=[smem] * 4 + [vmem] * 3 + [anywhere] * 3,
+        in_specs=[smem] * 4 + [vmem] * 6,
         out_specs=vmem,
         scratch_shapes=[
-            pltpu.VMEM((slots, rows, BLOCK), features.dtype),
-            pltpu.VMEM((own, 2 * rows, BLOCK), jnp.float32),
-            pltpu.SemaphoreType.DMA((3,)),
+            pltpu.VMEM((own + 2 * halo_low.shape[0], rows, BLOCK), features.dtype),
+            pltpu.VMEM((own, rows + 8, BLOCK), jnp.float32),
         ],
         compiler_params=pltpu.CompilerParams(vmem_limit_bytes=32 * 1024 * 1024),
         name="neighbour_mean",
@@ -154,18 +159,24 @@
     total = jnp.dot(w_self[...], whole(0), preferred_element_type=jnp.float32) + jnp.dot(
         w_neigh[...], whole(rows), preferred_element_type=jnp.float32
     )
-    updated = jnp.maximum(total + bias[...], 0.0).astype(out.dtype)
+    width = total.shape[0]
+    column = jnp.transpose(jnp.broadcast_to(bias[...], (width, width)))
+    total = total + jnp.concatenate([column] * (total.shape[1] // width), axis=1)
+    updated = jnp.maximum(total, 0.0).astype(out.dtype)
     for p in range(parts):
         out[p] = updated[p * rows : (p + 1) * rows]
 
 
 def project(shares, w_self, w_neigh, bias):
     parts, rows, width = shares.shape
+    vmem = pl.BlockSpec(memory_space=pltpu.VMEM)
     return pl.pallas_call(
         project_kernel,
         out_shape=jax.ShapeDtypeStruct((parts, rows // 2, width), shares.dtype),
+        in_specs=[vmem] * 4,
+        out_specs=vmem,
         name="project",
-    )(shares, w_self, w_neigh, bias[:, None])
+    )(shares, w_self, w_neigh, bias[None, :])
 
 
 def shards(

time: 107 us -> 101 us (0.944)
  blocking collectives: 58.6 us -> 73.3 us
  waiting for transfers between devices: 13.7 us -> 4.74 us
  Pallas kernels: 13.4 us -> 8.59 us
  starting transfers between devices: 15.7 us -> 11.3 us
  local copies, waits for them, and re-layouts: 4.1 us -> 1.91 us
    all_to_all x0 -> x1, blocking collectives: none -> 14.8 us  [shards(): shares = lax.all_to_all(shares, 'feat', 0, 0)]
    all_to_all x1 -> x0, waiting for transfers between devices: 8.95 us -> none  [shards(): shares = lax.all_to_all(shares, 'feat', 0, 0)]
    pallas_call x1, Pallas kernels: 9.69 us -> 4.91 us  [neighbour_mean(): pl.pallas_call(mean_kernel, out_shape=jax.ShapeDtypeStruct((parts, 2 * ro...]
    all_to_all x1 -> x0, starting transfers between devices: 4.48 us -> none  [shards(): shares = lax.all_to_all(shares, 'feat', 0, 0)]
    unnamed x18 -> x14, local copies, waits for them, and re-layouts: 1.48 us -> 0.03 us
  transfers between devices with their start and end apart: 4 -> 3, of which waited for: 3 -> 2; matrix products, arithmetic and copies ran while one was open for 1% -> 0% of each run, Pallas kernels for 0% -> 0%
where the time goes in v3:
time: 101 us
  blocking collectives  73.3 us (73%)
  starting transfers between devices  11.3 us (11%)
  Pallas kernels  8.59 us (9%)
  waiting for transfers between devices  4.74 us (5%)
  local copies, waits for them, and re-layouts  1.91 us (2%)
    all_gather x1, blocking collectives, shards(): column = lax.all_gather(hub_local, 'graph', axis_index_groups=along_z)  47.7 us
    all_to_all x1, blocking collectives, shards(): shares = lax.all_to_all(shares, 'feat', 0, 0)  14.8 us
    all_to_all x1, blocking collectives, shards(): lax.all_to_all(project(shares, w_self, w_neigh, bias), 'feat', 0, 0)  10.8 us
    all_to_all x1, starting transfers between devices, shards(): hub_rows = lax.all_to_all(spread, 'graph', 0, 0, axis_index_groups=nearby)  5.28 us
    pallas_call x1, Pallas kernels, neighbour_mean(): pl.pallas_call(mean_kernel, out_shape=jax.ShapeDtypeStruct((parts, 2 * ro...  4.91 us
    ppermute x1, starting transfers between devices, shards(): halo_low = lax.ppermute(outgoing[halo:], 'graph', forward)  3.5 us
    ppermute x1, waiting for transfers between devices, shards(): halo_high = lax.ppermute(outgoing[:halo], 'graph', backward)  2.83 us
    ppermute x1, starting transfers between devices, shards(): halo_high = lax.ppermute(outgoing[:halo], 'graph', backward)  2.47 us
  transfers between devices with their start and end apart: 3, of which 2 were waited for; matrix products, arithmetic and copies ran while one was open for 0% of the time, Pallas kernels for 0%

profile of v3, /device:TPU:6, one launch (start us, length us, event | category | flops | bytes accessed | tf_op | source)
XLA Modules:
  0.0 100.6 jit_solution(11571687677324559429)
XLA Ops:
  0.0 1.6 %pick_blocks.1 = (bf16[2,16,128]{2,1,0:T(8,128)(2,1)}, bf16[16,16,128]{2,1,0:T(8,128)(2,1)}) custom-call(s32[2]{0:T(128)} %hub_pick.1, s32[16]{0:T(128)} %halo_send.1, bf16[16,8192]{1,0:T(8,128)(2,1)} %features.3), custom_call_target="tpu_custom_call" | custom-call | tf_op jit(solution)/shard_map/pick_blocks/pallas_call | solution.py:28
  1.6 47.7 %all-gather = bf16[32,16,128]{2,1,0:T(8,128)(2,1)S(1)} all-gather(bf16[2,16,128]{2,1,0:T(8,128)(2,1)} %get-tuple-element.7), channel_id=2, replica_groups={{0,64,128,192,256,320,384,448,512,576,640,704,768,832,896,960},{8,72,13..., dimensions={0}, use_global_device_ids=true | all-gather | bytes 139264 | tf_op jit(solution)/shard_map/all_gather | solution.py:206
  49.3 1.2 %broadcast_in_dim.4 = bf16[8,16,2,16,128]{4,3,2,1,0:T(8,128)(2,1)} broadcast(bf16[16,2,16,128]{3,2,1,0:T(8,128)(2,1)S(1)} %bitcast.8), dimensions={1,2,3,4} | broadcast | bytes 1179648 | tf_op jit(solution)/shard_map/broadcast_in_dim | solution.py:207
  50.5 0.0 copy-start.6
  50.5 0.0 copy-start
  50.5 0.0 copy-start.2
  50.5 5.3 %all-to-all-start = ((bf16[8,16,2,16,128]{4,3,2,1,0:T(8,128)(2,1)}), bf16[8,16,2,16,128]{4,3,2,1,0:T(8,128)(2,1)S(1)}, u32[]{:S(2)}, u32[]{:S(2)}) async-start(bf16[8,16,2,16,128]{4,3,2,1,0:T(8,128)(2,1)} %broadcast_in_dim.4), calls=%async_computation | async-start | bytes 2097152 | tf_op jit(solution)/shard_map/all_to_all | solution.py:208
  55.8 0.0 copy-start.1
  55.8 0.0 copy-done.6
  55.8 3.5 %collective-permute-start = (bf16[8,16,128]{2,1,0:T(8,128)(2,1)S(1)}, bf16[8,16,128]{2,1,0:T(8,128)(2,1)S(1)}, u32[]{:S(2)}, u32[]{:S(2)}) collective-permute-start(bf16[8,16,128]{2,1,0:T(8,128)(2,1)S(1)} %get-tuple-element.10), channel_id=1, source_target_pairs={{0,8},{8,16},{16,24},{24,32},{32,40},{40,48},{48,56},{56,64},{64,7... | collective-permute-start | bytes 98312 | tf_op jit(solution)/shard_map/ppermute | solution.py:213
  59.3 2.5 %collective-permute-start.1 = (bf16[8,16,128]{2,1,0:T(8,128)(2,1)S(1)}, bf16[8,16,128]{2,1,0:T(8,128)(2,1)S(1)}, u32[]{:S(2)}, u32[]{:S(2)}) collective-permute-start(bf16[8,16,128]{2,1,0:T(8,128)(2,1)S(1)} %get-tuple-element.9), channel_id=1, source_target_pairs={{8,0},{16,8},{24,16},{32,24},{40,32},{48,40},{56,48},{64,56},{72,6... | collective-permute-start | bytes 98312 | tf_op jit(solution)/shard_map/ppermute | solution.py:214
  61.8 0.0 copy-start.4
  61.8 0.0 copy-start.5
  62.5 0.0 copy-start.3
  62.5 1.9 %collective-permute-done.halo_low = bf16[8,16,128]{2,1,0:T(8,128)(2,1)S(1)} collective-permute-done((bf16[8,16,128]{2,1,0:T(8,128)(2,1)S(1)}, bf16[8,16,128]{2,1,0:T(8,128)(2,1)S(1)}, u32[]{:S(2)}, u32[]{:S(2)}) %collective-permute-start) | collective-permute-done | bytes 32800 | tf_op jit(solution)/shard_map/ppermute | solution.py:213
  64.4 2.8 %collective-permute-done.1.halo_high = bf16[8,16,128]{2,1,0:T(8,128)(2,1)S(1)} collective-permute-done((bf16[8,16,128]{2,1,0:T(8,128)(2,1)S(1)}, bf16[8,16,128]{2,1,0:T(8,128)(2,1)S(1)}, u32[]{:S(2)}, u32[]{:S(2)}) %collective-permute-start.1) | collective-permute-done | bytes 32800 | tf_op jit(solution)/shard_map/ppermute | solution.py:214
  67.2 0.0 all-to-all-done
  67.2 0.0 copy-done
  67.2 0.0 copy-done.2
  67.2 0.0 copy-done.1
  67.2 0.0 copy-done.4
  67.3 0.0 copy-done.5
  67.3 0.0 copy-done.3
  67.3 4.9 %neighbour_mean.1 = bf16[8,32,1024]{2,1,0:T(8,128)(2,1)S(1)} custom-call(s32[256]{0:T(256)S(1)} %copy-done.3, s32[256]{0:T(256)S(1)} %copy-done.4, s32[256]{0:T(256)S(1)} %copy-done.5, s32[1]{0:T(128)S(6)} %copy.16.tile_count, bf16[16,8192]{1,0:T(8,128)(2,1)S(1)} %copy-done, s32[256,128]{1,0:T(8,128)S(1)} %copy-done.1, s32[256,128]{1,0:T(8,128)S(1)} %copy-done.2, ...), custom_call_target="tpu_custom_call" | custom-call | tf_op jit(solution)/shard_map/neighbour_mean/pallas_call | solution.py:139
  72.2 14.8 %all_to_all.15.shares = bf16[8,32,1024]{2,1,0:T(8,128)(2,1)} all-to-all(bf16[8,32,1024]{2,1,0:T(8,128)(2,1)S(1)} %neighbour_mean.1), channel_id=1, replica_groups=mesh['graph'=128,'feat'=8] {'feat'}, dimensions={0} | all-to-all | bytes 1048576 | tf_op jit(solution)/shard_map/all_to_all | solution.py:219
  87.0 2.1 %project.1 = bf16[8,16,1024]{2,1,0:T(8,128)(2,1)} custom-call(bf16[8,32,1024]{2,1,0:T(8,128)(2,1)} %all_to_all.15.shares, bf16[128,128]{1,0:T(8,128)(2,1)} %w_self.1, bf16[128,128]{1,0:T(8,128)(2,1)} %w_neigh.1, f32[1,128]{1,0:T(1,128)} %bitcast.9), custom_call_target="tpu_custom_call" | custom-call | tf_op jit(solution)/shard_map/project/pallas_call | solution.py:173
  89.0 10.8 %all_to_all.16 = bf16[8,16,1024]{2,1,0:T(8,128)(2,1)S(1)} all-to-all(bf16[8,16,1024]{2,1,0:T(8,128)(2,1)} %project.1), channel_id=1, replica_groups=mesh['graph'=128,'feat'=8] {'feat'}, dimensions={0} | all-to-all | bytes 524288 | tf_op jit(solution)/shard_map/all_to_all | solution.py:220
  99.9 0.7 copy.15
  (1 shorter events, 0.0 us)
Async XLA Ops:
  50.5 5.3 %copy-start.6 = (bf16[16,16,128]{2,1,0:T(8,128)(2,1)S(1)}, bf16[16,16,128]{2,1,0:T(8,128)(2,1)}, u32[]{:S(2)}) copy-start(bf16[16,16,128]{2,1,0:T(8,128)(2,1)} %get-tuple-element.8) | copy-start | bytes 196612
  50.5 16.7 %copy-start = (bf16[16,8192]{1,0:T(8,128)(2,1)S(1)}, bf16[16,8192]{1,0:T(8,128)(2,1)}, u32[]{:S(2)}) copy-start(bf16[16,8192]{1,0:T(8,128)(2,1)} %features.3) | copy-start | bytes 786436
  50.5 16.7 %copy-start.2 = (s32[256,128]{1,0:T(8,128)S(1)}, s32[256,128]{1,0:T(8,128)}, u32[]{:S(2)}) copy-start(s32[256,128]{1,0:T(8,128)} %edge_dst.1) | copy-start | bytes 393220
  50.5 16.7 %all-to-all-start = ((bf16[8,16,2,16,128]{4,3,2,1,0:T(8,128)(2,1)}), bf16[8,16,2,16,128]{4,3,2,1,0:T(8,128)(2,1)S(1)}, u32[]{:S(2)}, u32[]{:S(2)}) async-start(bf16[8,16,2,16,128]{4,3,2,1,0:T(8,128)(2,1)} %broadcast_in_dim.4), calls=%async_computation | async-start | bytes 2097152 | tf_op jit(solution)/shard_map/all_to_all | solution.py:208
  55.8 11.5 %copy-start.1 = (s32[256,128]{1,0:T(8,128)S(1)}, s32[256,128]{1,0:T(8,128)}, u32[]{:S(2)}) copy-start(s32[256,128]{1,0:T(8,128)} %edge_src.1) | copy-start | bytes 393220
  55.8 8.6 %collective-permute-start = (bf16[8,16,128]{2,1,0:T(8,128)(2,1)S(1)}, bf16[8,16,128]{2,1,0:T(8,128)(2,1)S(1)}, u32[]{:S(2)}, u32[]{:S(2)}) collective-permute-start(bf16[8,16,128]{2,1,0:T(8,128)(2,1)S(1)} %get-tuple-element.10), channel_id=1, source_target_pairs={{0,8},{8,16},{16,24},{24,32},{32,40},{40,48},{48,56},{56,64},{64,7... | collective-permute-start | bytes 98312 | tf_op jit(solution)/shard_map/ppermute | solution.py:213
  59.3 7.9 %collective-permute-start.1 = (bf16[8,16,128]{2,1,0:T(8,128)(2,1)S(1)}, bf16[8,16,128]{2,1,0:T(8,128)(2,1)S(1)}, u32[]{:S(2)}, u32[]{:S(2)}) collective-permute-start(bf16[8,16,128]{2,1,0:T(8,128)(2,1)S(1)} %get-tuple-element.9), channel_id=1, source_target_pairs={{8,0},{16,8},{24,16},{32,24},{40,32},{48,40},{56,48},{64,56},{72,6... | collective-permute-start | bytes 98312 | tf_op jit(solution)/shard_map/ppermute | solution.py:214
  61.8 5.5 %copy-start.4 = (s32[256]{0:T(256)S(1)}, s32[256]{0:T(256)}, u32[]{:S(2)}) copy-start(s32[256]{0:T(256)} %tile_src.1) | copy-start | bytes 3076
  61.8 5.5 %copy-start.5 = (s32[256]{0:T(256)S(1)}, s32[256]{0:T(256)}, u32[]{:S(2)}) copy-start(s32[256]{0:T(256)} %tile_edges.1) | copy-start | bytes 3076
  62.5 4.8 %copy-start.3 = (s32[256]{0:T(256)S(1)}, s32[256]{0:T(256)}, u32[]{:S(2)}) copy-start(s32[256]{0:T(256)} %tile_dst.1) | copy-start | bytes 3076

commit v4 on v3

--- a/solution.py
+++ b/solution.py
@@ -6,19 +6,20 @@
 from jax.sharding import PartitionSpec as P
 
 BLOCK = 128
-GROUP = 32
+GROUP = 64
 Z, X = 32, 4
 STRIDE = 2
 
 
-def pick_kernel(hub_pick, halo_send, features, hub_out, halo_out):
-    def copy(out, picks):
+def pick_kernel(hub_pick, halo_send, features, hub_out, before_out, after_out):
+    def copy(out, picks, first):
         for i in range(out.shape[0]):
-            start = pl.multiple_of(picks[i] * BLOCK, BLOCK)
+            start = pl.multiple_of(picks[first + i] * BLOCK, BLOCK)
             out[i] = features[:, pl.ds(start, BLOCK)]
 
-    copy(hub_out, hub_pick)
-    copy(halo_out, halo_send)
+    copy(hub_out, hub_pick, 0)
+    copy(before_out, halo_send, 0)
+    copy(after_out, halo_send, before_out.shape[0])
 
 
 def pick_blocks(features, hub_pick, halo_send):
@@ -29,10 +30,11 @@
         pick_kernel,
         out_shape=[
             jax.ShapeDtypeStruct((hub_pick.shape[0], rows, BLOCK), features.dtype),
-            jax.ShapeDtypeStruct((halo_send.shape[0], rows, BLOCK), features.dtype),
+            jax.ShapeDtypeStruct((halo_send.shape[0] // 2, rows, BLOCK), features.dtype),
+            jax.ShapeDtypeStruct((halo_send.shape[0] // 2, rows, BLOCK), features.dtype),
         ],
         in_specs=[smem, smem, vmem],
-        out_specs=[vmem, vmem],
+        out_specs=[vmem] * 3,
         name="pick_blocks",
     )(hub_pick, halo_send, features)
 
@@ -44,10 +46,7 @@
 
 
 def mean_kernel(
-    tile_dst,
-    tile_src,
-    tile_edges,
-    tile_count,
+    plan,
     features,
     edge_src,
     edge_dst,
@@ -60,7 +59,6 @@
 ):
     rows = features.shape[0]
     own = features.shape[1] // BLOCK
-    hubs = hub_rows.shape[0]
     halo = halo_low.shape[0]
     for b in range(own):
         table[b] = features[:, b * BLOCK : (b + 1) * BLOCK]
@@ -69,12 +67,16 @@
         table[own + b] = halo_low[b]
         table[own + halo + b] = halo_high[b]
 
-    count = tile_count[0]
+    slots = edge_src.shape[0]
+    tile_dst, tile_near, tile_far, tile_live = (plan.at[pl.ds(i * slots, slots)] for i in range(4))
+    count = plan[4 * slots]
     lane = lax.broadcasted_iota(jnp.int32, (8, BLOCK), 1)
     node = lax.broadcasted_iota(jnp.int32, (BLOCK, BLOCK), 0).astype(jnp.bfloat16)
     one, zero = jnp.ones((), jnp.bfloat16), jnp.zeros((), jnp.bfloat16)
-    ones = jnp.ones((rows, BLOCK), jnp.bfloat16)
-    blank = jnp.zeros((2 * rows, BLOCK), jnp.bfloat16)
+    blank = jnp.zeros((rows, BLOCK), jnp.bfloat16)
+    upper = lax.broadcasted_iota(jnp.int32, (16, 2 * BLOCK), 0) < 8
+    first_tile = lax.broadcasted_iota(jnp.int32, (16, 2 * BLOCK), 1) < BLOCK
+    ones = jnp.where(upper == first_tile, 1.0, 0.0).astype(jnp.bfloat16)
 
     @pl.loop(0, (count + GROUP - 1) // GROUP)
     def _(step):
@@ -84,21 +86,16 @@
         lefts, rights, parts = [], [], []
         for i in range(GROUP):
             tile = first + i
-            slot = tile_src[tile]
-            hub = slot - own
-            is_hub = (hub >= 0) & (hub < hubs)
-            near = table[jnp.where(is_hub, 0, jnp.where(hub < 0, slot, slot - hubs))]
-            far = hub_rows[jnp.where(is_hub, hub_row(hub, hubs), 0)]
-            block = jnp.where(is_hub, far, near).astype(jnp.float32)
+            far = tile_far[tile]
+            block = jnp.where(far >= 0, hub_rows[jnp.maximum(far, 0)], table[tile_near[tile]])
+            block = block.astype(jnp.float32)
             index = jnp.broadcast_to(sources[i : i + 1], (8, BLOCK))
             values = [
                 jnp.take_along_axis(block[r : r + 8], index, axis=1, mode="promise_in_bounds")
                 for r in range(0, rows, 8)
             ]
-            values = jnp.concatenate(values, axis=0).astype(jnp.bfloat16)
-            lefts.append(jnp.concatenate([values, ones], axis=0))
-            live = jnp.where(tile < count, tile_edges[tile], 0)
-            target = jnp.where(lane < live, jnp.broadcast_to(targets[i : i + 1], (8, BLOCK)), -1)
+            lefts.append(jnp.concatenate(values, axis=0).astype(jnp.bfloat16))
+            target = jnp.where(lane < tile_live[tile], jnp.broadcast_to(targets[i : i + 1], (8, BLOCK)), -1)
             hits = node == jnp.broadcast_to(target[:1].astype(jnp.bfloat16), (BLOCK, BLOCK))
             rights.append(jnp.where(hits, one, zero))
         for i in range(0, GROUP, 2):
@@ -106,6 +103,7 @@
                 [
                     jnp.concatenate([lefts[i], blank], axis=1),
                     jnp.concatenate([blank, lefts[i + 1]], axis=1),
+                    ones,
                 ],
                 axis=0,
             )
@@ -113,8 +111,10 @@
             both = lax.dot_general(
                 left, right, (((1,), (1,)), ((), ())), preferred_element_type=jnp.float32
             )
-            parts.append(both[: rows + 8])
-            parts.append(both[2 * rows : 3 * rows + 8])
+            for k in range(2):
+                values = both[k * rows : (k + 1) * rows]
+                degrees = both[2 * rows + 8 * k : 2 * rows + 8 * (k + 1)]
+                parts.append(jnp.concatenate([values, degrees], axis=0))
         for i in range(GROUP):
             place = tile_dst[first + i]
             sums[place] = sums[place] + parts[i]
@@ -134,12 +134,19 @@
 ):
     rows, nodes = features.shape
     own = nodes // BLOCK
+    hubs = hub_rows.shape[0]
+    hub = tile_src - own
+    is_hub = (hub >= 0) & (hub < hubs)
+    tile_near = jnp.where(is_hub, 0, jnp.where(hub < 0, tile_src, tile_src - hubs))
+    tile_far = jnp.where(is_hub, hub_row(hub, hubs), -1)
+    tile_live = jnp.where(jnp.arange(tile_src.shape[0], dtype=jnp.int32) < tile_count[0], tile_edges, 0)
+    plan = jnp.concatenate([tile_dst, tile_near, tile_far, tile_live, tile_count])
     smem = pl.BlockSpec(memory_space=pltpu.SMEM)
     vmem = pl.BlockSpec(memory_space=pltpu.VMEM)
     return pl.pallas_call(
         mean_kernel,
         out_shape=jax.ShapeDtypeStruct((parts, 2 * rows, nodes // parts), features.dtype),
-        in_specs=[smem] * 4 + [vmem] * 6,
+        in_specs=[smem] + [vmem] * 6,
         out_specs=vmem,
         scratch_shapes=[
             pltpu.VMEM((own + 2 * halo_low.shape[0], rows, BLOCK), features.dtype),
@@ -147,7 +154,7 @@
         ],
         compiler_params=pltpu.CompilerParams(vmem_limit_bytes=32 * 1024 * 1024),
         name="neighbour_mean",
-    )(tile_dst, tile_src, tile_edges, tile_count, features, edge_src, edge_dst, hub_rows, halo_low, halo_high)
+    )(plan, features, edge_src, edge_dst, hub_rows, halo_low, halo_high)
 
 
 def project_kernel(shares, w_self, w_neigh, bias, out):
@@ -196,22 +203,22 @@
     rows, nodes = features.shape
     parts = lax.axis_size("feat")
     count = lax.axis_size("graph")
-    halo = halo_send.shape[0] // 2
-    hub_local, outgoing = pick_blocks(features, hub_pick, halo_send)
+    hub_local, to_previous, to_next = pick_blocks(features, hub_pick, halo_send)
 
     along_z = [[X * z + x for z in range(r, Z, STRIDE)] for r in range(STRIDE) for x in range(X)]
     nearby = [
         [X * (z + r) + x for r in range(STRIDE) for x in range(X)] for z in range(0, Z, STRIDE)
     ]
     column = lax.all_gather(hub_local, "graph", axis_index_groups=along_z)
+    column, tile_src, tile_edges = lax.optimization_barrier((column, tile_src, tile_edges))
     spread = jnp.broadcast_to(column[None], (X * STRIDE, *column.shape))
     hub_rows = lax.all_to_all(spread, "graph", 0, 0, axis_index_groups=nearby)
     hub_rows = hub_rows.reshape(-1, rows, BLOCK)
 
     forward = [(i, (i + 1) % count) for i in range(count)]
     backward = [(target, source) for source, target in forward]
-    halo_low = lax.ppermute(outgoing[halo:], "graph", forward)
-    halo_high = lax.ppermute(outgoing[:halo], "graph", backward)
+    halo_low = lax.ppermute(to_next, "graph", forward)
+    halo_high = lax.ppermute(to_previous, "graph", backward)
 
     shares = neighbour_mean(
         features, hub_rows, halo_low, halo_high, tile_dst, tile_src, tile_edges, tile_count, edge_src, edge_dst, parts

time: 101 us -> 100 us (0.990)
  waiting for transfers between devices: 4.74 us -> 3.35 us
  local copies, waits for them, and re-layouts: 1.91 us -> 3.25 us
    ppermute x2, waiting for transfers between devices: 4.74 us -> 3.35 us  [the longest x1 2.68 us: shards(): halo_high = lax.ppermute(to_previous, 'graph', backward)]
    unnamed x14 -> x17, local copies, waits for them, and re-layouts: 0.03 us -> 1.37 us
where the time goes in v4:
time: 100 us; the launch traced here: 99.9 us
  blocking collectives  73.3 us (73%)
  starting transfers between devices  11.1 us (11%)
  Pallas kernels  8.01 us (8%)
  waiting for transfers between devices  3.35 us (3%)
  local copies, waits for them, and re-layouts  3.25 us (3%)
    all_gather x1, blocking collectives, shards(): column = lax.all_gather(hub_local, 'graph', axis_index_groups=along_z)  47.7 us
    all_to_all x1, blocking collectives, shards(): shares = lax.all_to_all(shares, 'feat', 0, 0)  14.8 us
    all_to_all x1, blocking collectives, shards(): lax.all_to_all(project(shares, w_self, w_neigh, bias), 'feat', 0, 0)  10.8 us
    all_to_all x1, starting transfers between devices, shards(): hub_rows = lax.all_to_all(spread, 'graph', 0, 0, axis_index_groups=nearby)  5.29 us
    pallas_call x1, Pallas kernels, neighbour_mean(): pl.pallas_call(mean_kernel, out_shape=jax.ShapeDtypeStruct((parts, 2 * ro...  4.34 us
    ppermute x1, starting transfers between devices, shards(): halo_low = lax.ppermute(to_next, 'graph', forward)  3.36 us
    ppermute x1, waiting for transfers between devices, shards(): halo_high = lax.ppermute(to_previous, 'graph', backward)  2.68 us
    ppermute x1, starting transfers between devices, shards(): halo_high = lax.ppermute(to_previous, 'graph', backward)  2.47 us
  transfers between devices with their start and end apart: 3, of which 2 were waited for; matrix products, arithmetic and copies ran while one was open for 0% of the time, Pallas kernels for 0%

profile of v4, /device:TPU:6, one launch (start us, length us, event | category | flops | bytes accessed | tf_op | source)
XLA Modules:
  0.0 99.9 jit_solution(12429324788584985616)
XLA Ops:
  0.0 1.6 %pick_blocks.1 = (bf16[2,16,128]{2,1,0:T(8,128)(2,1)}, bf16[8,16,128]{2,1,0:T(8,128)(2,1)}, bf16[8,16,128]{2,1,0:T(8,128)(2,1)}) custom-call(s32[2]{0:T(128)} %hub_pick.1, s32[16]{0:T(128)} %halo_send.1, bf16[16,8192]{1,0:T(8,128)(2,1)} %features.3), custom_call_target="tpu_custom_call" | custom-call | tf_op jit(solution)/shard_map/pick_blocks/pallas_call | solution.py:29
  1.6 47.7 %all-gather = bf16[32,16,128]{2,1,0:T(8,128)(2,1)S(1)} all-gather(bf16[2,16,128]{2,1,0:T(8,128)(2,1)} %get-tuple-element.11), channel_id=2, replica_groups={{0,64,128,192,256,320,384,448,512,576,640,704,768,832,896,960},{8,72,13..., dimensions={0}, use_global_device_ids=true | all-gather | bytes 139264 | tf_op jit(solution)/shard_map/all_gather | solution.py:212
  49.3 1.2 %broadcast_in_dim.14 = bf16[8,16,2,16,128]{4,3,2,1,0:T(8,128)(2,1)} broadcast(bf16[16,2,16,128]{3,2,1,0:T(8,128)(2,1)S(1)} %bitcast.10), dimensions={1,2,3,4} | broadcast | bytes 1179648 | tf_op jit(solution)/shard_map/broadcast_in_dim | solution.py:214
  50.5 0.0 copy-start.7
  50.5 0.0 copy-start.6
  50.5 0.0 copy-start
  50.5 0.0 copy-start.1
  50.5 0.0 copy-start.2
  50.5 5.3 %all-to-all-start = ((bf16[8,16,2,16,128]{4,3,2,1,0:T(8,128)(2,1)}), bf16[8,16,2,16,128]{4,3,2,1,0:T(8,128)(2,1)S(1)}, u32[]{:S(2)}, u32[]{:S(2)}) async-start(bf16[8,16,2,16,128]{4,3,2,1,0:T(8,128)(2,1)} %broadcast_in_dim.14), calls=%async_computation | async-start | bytes 2097152 | tf_op jit(solution)/shard_map/all_to_all | solution.py:215
  55.8 0.0 copy-done.7
  55.8 3.4 %collective-permute-start = (bf16[8,16,128]{2,1,0:T(8,128)(2,1)S(1)}, bf16[8,16,128]{2,1,0:T(8,128)(2,1)S(1)}, u32[]{:S(2)}, u32[]{:S(2)}) collective-permute-start(bf16[8,16,128]{2,1,0:T(8,128)(2,1)S(1)} %copy-done.7), channel_id=1, source_target_pairs={{0,8},{8,16},{16,24},{24,32},{32,40},{40,48},{48,56},{56,64},{64,7... | collective-permute-start | bytes 98312 | tf_op jit(solution)/shard_map/ppermute | solution.py:220
  59.2 0.0 copy-done.6
  59.2 2.5 %collective-permute-start.1 = (bf16[8,16,128]{2,1,0:T(8,128)(2,1)S(1)}, bf16[8,16,128]{2,1,0:T(8,128)(2,1)S(1)}, u32[]{:S(2)}, u32[]{:S(2)}) collective-permute-start(bf16[8,16,128]{2,1,0:T(8,128)(2,1)S(1)} %copy-done.6), channel_id=1, source_target_pairs={{8,0},{16,8},{24,16},{32,24},{40,32},{48,40},{56,48},{64,56},{72,6... | collective-permute-start | bytes 98312 | tf_op jit(solution)/shard_map/ppermute | solution.py:221
  61.7 0.0 copy-start.4
  62.3 0.0 copy-done.4
  62.4 0.0 copy-start.3
  62.4 0.7 copy-done.3
  63.1 0.0 copy-start.5
  63.1 0.7 copy-done.5
  63.8 0.7 collective-permute-done.halo_low
  64.4 2.7 %collective-permute-done.1.halo_high = bf16[8,16,128]{2,1,0:T(8,128)(2,1)S(1)} collective-permute-done((bf16[8,16,128]{2,1,0:T(8,128)(2,1)S(1)}, bf16[8,16,128]{2,1,0:T(8,128)(2,1)S(1)}, u32[]{:S(2)}, u32[]{:S(2)}) %collective-permute-start.1) | collective-permute-done | bytes 32800 | tf_op jit(solution)/shard_map/ppermute | solution.py:221
  67.1 0.0 all-to-all-done
  67.1 0.0 copy-done
  67.1 0.0 copy-done.1
  67.1 0.0 copy-done.2
  67.1 4.3 %neighbour_mean.1 = bf16[8,32,1024]{2,1,0:T(8,128)(2,1)S(1)} custom-call(s32[1025]{0:T(1024)S(1)} %constant_dynamic-update-slice_fusion.plan, bf16[16,8192]{1,0:T(8,128)(2,1)S(1)} %copy-done, s32[256,128]{1,0:T(8,128)S(1)} %copy-done.1, s32[256,128]{1,0:T(8,128)S(1)} %copy-done.2, bf16[256,16,128]{2,1,0:T(8,128)(2,1)S(1)} %bitcast.8, ...), custom_call_target="tpu_custom_call" | custom-call | tf_op jit(solution)/shard_map/neighbour_mean/pallas_call | solution.py:146
  71.5 14.8 %all_to_all.15.shares = bf16[8,32,1024]{2,1,0:T(8,128)(2,1)} all-to-all(bf16[8,32,1024]{2,1,0:T(8,128)(2,1)S(1)} %neighbour_mean.1), channel_id=1, replica_groups=mesh['graph'=128,'feat'=8] {'feat'}, dimensions={0} | all-to-all | bytes 1048576 | tf_op jit(solution)/shard_map/all_to_all | solution.py:226
  86.2 2.1 %project.1 = bf16[8,16,1024]{2,1,0:T(8,128)(2,1)} custom-call(bf16[8,32,1024]{2,1,0:T(8,128)(2,1)} %all_to_all.15.shares, bf16[128,128]{1,0:T(8,128)(2,1)} %w_self.1, bf16[128,128]{1,0:T(8,128)(2,1)} %w_neigh.1, f32[1,128]{1,0:T(1,128)} %bitcast.11), custom_call_target="tpu_custom_call" | custom-call | tf_op jit(solution)/shard_map/project/pallas_call | solution.py:180
  88.3 10.8 %all_to_all.16 = bf16[8,16,1024]{2,1,0:T(8,128)(2,1)S(1)} all-to-all(bf16[8,16,1024]{2,1,0:T(8,128)(2,1)} %project.1), channel_id=1, replica_groups=mesh['graph'=128,'feat'=8] {'feat'}, dimensions={0} | all-to-all | bytes 524288 | tf_op jit(solution)/shard_map/all_to_all | solution.py:227
  99.1 0.7 copy.15
  (6 shorter events, 0.0 us)
Async XLA Ops:
  50.5 5.3 %copy-start.7 = (bf16[8,16,128]{2,1,0:T(8,128)(2,1)S(1)}, bf16[8,16,128]{2,1,0:T(8,128)(2,1)}, u32[]{:S(2)}) copy-start(bf16[8,16,128]{2,1,0:T(8,128)(2,1)} %get-tuple-element.15) | copy-start | bytes 98308
  50.5 8.7 %copy-start.6 = (bf16[8,16,128]{2,1,0:T(8,128)(2,1)S(1)}, bf16[8,16,128]{2,1,0:T(8,128)(2,1)}, u32[]{:S(2)}) copy-start(bf16[8,16,128]{2,1,0:T(8,128)(2,1)} %get-tuple-element.16) | copy-start | bytes 98308
  50.5 16.6 %copy-start = (bf16[16,8192]{1,0:T(8,128)(2,1)S(1)}, bf16[16,8192]{1,0:T(8,128)(2,1)}, u32[]{:S(2)}) copy-start(bf16[16,8192]{1,0:T(8,128)(2,1)} %features.3) | copy-start | bytes 786436
  50.5 16.6 %copy-start.1 = (s32[256,128]{1,0:T(8,128)S(1)}, s32[256,128]{1,0:T(8,128)}, u32[]{:S(2)}) copy-start(s32[256,128]{1,0:T(8,128)} %edge_src.1) | copy-start | bytes 393220
  50.5 16.6 %copy-start.2 = (s32[256,128]{1,0:T(8,128)S(1)}, s32[256,128]{1,0:T(8,128)}, u32[]{:S(2)}) copy-start(s32[256,128]{1,0:T(8,128)} %edge_dst.1) | copy-start | bytes 393220
  50.5 16.6 %all-to-all-start = ((bf16[8,16,2,16,128]{4,3,2,1,0:T(8,128)(2,1)}), bf16[8,16,2,16,128]{4,3,2,1,0:T(8,128)(2,1)S(1)}, u32[]{:S(2)}, u32[]{:S(2)}) async-start(bf16[8,16,2,16,128]{4,3,2,1,0:T(8,128)(2,1)} %broadcast_in_dim.14), calls=%async_computation | async-start | bytes 2097152 | tf_op jit(solution)/shard_map/all_to_all | solution.py:215
  55.8 8.6 %collective-permute-start = (bf16[8,16,128]{2,1,0:T(8,128)(2,1)S(1)}, bf16[8,16,128]{2,1,0:T(8,128)(2,1)S(1)}, u32[]{:S(2)}, u32[]{:S(2)}) collective-permute-start(bf16[8,16,128]{2,1,0:T(8,128)(2,1)S(1)} %copy-done.7), channel_id=1, source_target_pairs={{0,8},{8,16},{16,24},{24,32},{32,40},{40,48},{48,56},{56,64},{64,7... | collective-permute-start | bytes 98312 | tf_op jit(solution)/shard_map/ppermute | solution.py:220
  59.2 7.9 %collective-permute-start.1 = (bf16[8,16,128]{2,1,0:T(8,128)(2,1)S(1)}, bf16[8,16,128]{2,1,0:T(8,128)(2,1)S(1)}, u32[]{:S(2)}, u32[]{:S(2)}) collective-permute-start(bf16[8,16,128]{2,1,0:T(8,128)(2,1)S(1)} %copy-done.6), channel_id=1, source_target_pairs={{8,0},{16,8},{24,16},{32,24},{40,32},{48,40},{56,48},{64,56},{72,6... | collective-permute-start | bytes 98312 | tf_op jit(solution)/shard_map/ppermute | solution.py:221
  61.7 0.7 copy-start.4
  62.4 0.7 copy-start.3
  63.1 0.7 copy-start.5

commit v5 on v4

--- a/solution.py
+++ b/solution.py
@@ -157,33 +157,11 @@
     )(plan, features, edge_src, edge_dst, hub_rows, halo_low, halo_high)
 
 
-def project_kernel(shares, w_self, w_neigh, bias, out):
-    parts, rows, _ = out.shape
-
-    def whole(first):
-        return jnp.concatenate([shares[p, first : first + rows] for p in range(parts)], axis=0)
-
-    total = jnp.dot(w_self[...], whole(0), preferred_element_type=jnp.float32) + jnp.dot(
-        w_neigh[...], whole(rows), preferred_element_type=jnp.float32
-    )
-    width = total.shape[0]
-    column = jnp.transpose(jnp.broadcast_to(bias[...], (width, width)))
-    total = total + jnp.concatenate([column] * (total.shape[1] // width), axis=1)
-    updated = jnp.maximum(total, 0.0).astype(out.dtype)
-    for p in range(parts):
-        out[p] = updated[p * rows : (p + 1) * rows]
-
-
-def project(shares, w_self, w_neigh, bias):
+def project(shares, weights, bias):
     parts, rows, width = shares.shape
-    vmem = pl.BlockSpec(memory_space=pltpu.VMEM)
-    return pl.pallas_call(
-        project_kernel,
-        out_shape=jax.ShapeDtypeStruct((parts, rows // 2, width), shares.dtype),
-        in_specs=[vmem] * 4,
-        out_specs=vmem,
-        name="project",
-    )(shares, w_self, w_neigh, bias[None, :])
+    total = jnp.dot(weights, shares.reshape(parts * rows, width), preferred_element_type=jnp.float32)
+    updated = jnp.maximum(total + bias[:, None], 0.0).astype(shares.dtype)
+    return updated.reshape(parts, rows // 2, width)
 
 
 def shards(
@@ -210,7 +188,12 @@
         [X * (z + r) + x for r in range(STRIDE) for x in range(X)] for z in range(0, Z, STRIDE)
     ]
     column = lax.all_gather(hub_local, "graph", axis_index_groups=along_z)
-    column, tile_src, tile_edges = lax.optimization_barrier((column, tile_src, tile_edges))
+    column, tile_src, tile_edges, w_self, w_neigh = lax.optimization_barrier(
+        (column, tile_src, tile_edges, w_self, w_neigh)
+    )
+    weights = jnp.stack(
+        [w_self.reshape(-1, parts, rows), w_neigh.reshape(-1, parts, rows)], axis=2
+    ).reshape(-1, 2 * parts * rows)
     spread = jnp.broadcast_to(column[None], (X * STRIDE, *column.shape))
     hub_rows = lax.all_to_all(spread, "graph", 0, 0, axis_index_groups=nearby)
     hub_rows = hub_rows.reshape(-1, rows, BLOCK)
@@ -220,11 +203,12 @@
     halo_low = lax.ppermute(to_next, "graph", forward)
     halo_high = lax.ppermute(to_previous, "graph", backward)
 
+    hub_rows, weights = lax.optimization_barrier((hub_rows, weights))
     shares = neighbour_mean(
         features, hub_rows, halo_low, halo_high, tile_dst, tile_src, tile_edges, tile_count, edge_src, edge_dst, parts
     )
     shares = lax.all_to_all(shares, "feat", 0, 0)
-    updated = lax.all_to_all(project(shares, w_self, w_neigh, bias), "feat", 0, 0)
+    updated = lax.all_to_all(project(shares, weights, bias), "feat", 0, 0)
     return jnp.transpose(updated, (1, 0, 2)).reshape(rows, nodes)
 
 

time: 100 us -> 97.4 us (0.974)
  Pallas kernels: 8.01 us -> 5.06 us
  waiting for transfers between devices: 3.35 us -> 4.36 us
  blocking collectives: 73.3 us -> 72.3 us
    all_to_all x1, waiting for transfers between devices: 0.01 us -> 2.45 us  [shards(): hub_rows = lax.all_to_all(spread, 'graph', 0, 0, axis_index_groups=nearby)]
    pallas_call x1 -> x0, Pallas kernels: 2.06 us -> none  [project(): pl.pallas_call(project_kernel, out_shape=jax.ShapeDtypeStruct((parts, row...]
where the time goes in v5:
time: 97.4 us; the launch traced here: 97 us
  blocking collectives  72.3 us (74%)
  starting transfers between devices  11.3 us (12%)
  Pallas kernels  5.06 us (5%)
  waiting for transfers between devices  4.36 us (4%)
  local copies, waits for them, and re-layouts  2.82 us (3%)
    all_gather x1, blocking collectives, shards(): column = lax.all_gather(hub_local, 'graph', axis_index_groups=along_z)  47.7 us
    all_to_all x1, blocking collectives, shards(): shares = lax.all_to_all(shares, 'feat', 0, 0)  14.7 us
    all_to_all x1, blocking collectives, shards(): updated = lax.all_to_all(project(shares, weights, bias), 'feat', 0, 0)  9.95 us
    all_to_all x1, starting transfers between devices, shards(): hub_rows = lax.all_to_all(spread, 'graph', 0, 0, axis_index_groups=nearby)  5.29 us
    ppermute x1, starting transfers between devices, shards(): halo_low = lax.ppermute(to_next, 'graph', forward)  3.5 us
    pallas_call x1, Pallas kernels, neighbour_mean(): pl.pallas_call(mean_kernel, out_shape=jax.ShapeDtypeStruct((parts, 2 * ro...  3.46 us
    ppermute x1, starting transfers between devices, shards(): halo_high = lax.ppermute(to_previous, 'graph', backward)  2.47 us
    all_to_all x1, waiting for transfers between devices, shards(): hub_rows = lax.all_to_all(spread, 'graph', 0, 0, axis_index_groups=nearby)  2.45 us
  transfers between devices with their start and end apart: 3, of which 2 were waited for; matrix products, arithmetic and copies ran while one was open for 0% of the time, Pallas kernels for 0%

profile of v5, /device:TPU:6, one launch (start us, length us, event | category | flops | bytes accessed | tf_op | source)
XLA Modules:
  0.0 97.0 jit_solution(8077578166383655948)
XLA Ops:
  0.0 1.6 %pick_blocks.1 = (bf16[2,16,128]{2,1,0:T(8,128)(2,1)}, bf16[8,16,128]{2,1,0:T(8,128)(2,1)}, bf16[8,16,128]{2,1,0:T(8,128)(2,1)}) custom-call(s32[2]{0:T(128)} %hub_pick.1, s32[16]{0:T(128)} %halo_send.1, bf16[16,8192]{1,0:T(8,128)(2,1)} %features.3), custom_call_target="tpu_custom_call" | custom-call | tf_op jit(solution)/shard_map/pick_blocks/pallas_call | solution.py:29
  1.6 47.7 %all-gather = bf16[32,16,128]{2,1,0:T(8,128)(2,1)S(1)} all-gather(bf16[2,16,128]{2,1,0:T(8,128)(2,1)} %get-tuple-element.15), channel_id=2, replica_groups={{0,64,128,192,256,320,384,448,512,576,640,704,768,832,896,960},{8,72,13..., dimensions={0}, use_global_device_ids=true | all-gather | bytes 139264 | tf_op jit(solution)/shard_map/all_gather | solution.py:190
  49.3 1.2 %broadcast_in_dim.6 = bf16[8,16,2,16,128]{4,3,2,1,0:T(8,128)(2,1)} broadcast(bf16[16,2,16,128]{3,2,1,0:T(8,128)(2,1)S(1)} %bitcast.18), dimensions={1,2,3,4} | broadcast | bytes 1179648 | tf_op jit(solution)/shard_map/broadcast_in_dim | solution.py:197
  50.5 0.0 copy-start.6
  50.5 0.0 copy-start.5
  50.5 0.0 copy-start.7
  50.5 0.0 copy-start.2
  50.5 5.3 %all-to-all-start = ((bf16[8,16,2,16,128]{4,3,2,1,0:T(8,128)(2,1)}), bf16[8,16,2,16,128]{4,3,2,1,0:T(8,128)(2,1)S(1)}, u32[]{:S(2)}, u32[]{:S(2)}) async-start(bf16[8,16,2,16,128]{4,3,2,1,0:T(8,128)(2,1)} %broadcast_in_dim.6), calls=%async_computation | async-start | bytes 2097152 | tf_op jit(solution)/shard_map/all_to_all | solution.py:198
  55.8 0.0 copy-done.10
  55.8 3.5 %collective-permute-start = (bf16[8,16,128]{2,1,0:T(8,128)(2,1)S(1)}, bf16[8,16,128]{2,1,0:T(8,128)(2,1)S(1)}, u32[]{:S(2)}, u32[]{:S(2)}) collective-permute-start(bf16[8,16,128]{2,1,0:T(8,128)(2,1)S(1)} %copy-done.10), channel_id=1, source_target_pairs={{0,8},{8,16},{16,24},{24,32},{32,40},{40,48},{48,56},{56,64},{64,7... | collective-permute-start | bytes 98312 | tf_op jit(solution)/shard_map/ppermute | solution.py:203
  59.3 0.0 copy-done.9
  59.4 2.5 %collective-permute-start.1 = (bf16[8,16,128]{2,1,0:T(8,128)(2,1)S(1)}, bf16[8,16,128]{2,1,0:T(8,128)(2,1)S(1)}, u32[]{:S(2)}, u32[]{:S(2)}) collective-permute-start(bf16[8,16,128]{2,1,0:T(8,128)(2,1)S(1)} %copy-done.9), channel_id=1, source_target_pairs={{8,0},{16,8},{24,16},{32,24},{40,32},{48,40},{56,48},{64,56},{72,6... | collective-permute-start | bytes 98312 | tf_op jit(solution)/shard_map/ppermute | solution.py:204
  61.8 0.0 copy-done.3
  61.9 0.1 copy.19
  62.0 0.0 copy-done.4
  62.0 0.1 copy.18
  62.8 0.0 copy-done.6
  62.8 0.0 copy-done.5
  62.8 0.0 copy-done.7
  62.9 0.0 copy-start.1
  62.9 2.4 %all-to-all-done = bf16[8,16,2,16,128]{4,3,2,1,0:T(8,128)(2,1)S(1)} async-done(((bf16[8,16,2,16,128]{4,3,2,1,0:T(8,128)(2,1)}), bf16[8,16,2,16,128]{4,3,2,1,0:T(8,128)(2,1)S(1)}, u32[]{:S(2)}, u32[]{:S(2)}) %all-to-all-start) | async-done | bytes 1048608 | tf_op jit(solution)/shard_map/all_to_all | solution.py:198
  65.4 0.0 collective-permute-done.halo_low
  65.4 1.9 %collective-permute-done.1.halo_high = bf16[8,16,128]{2,1,0:T(8,128)(2,1)S(1)} collective-permute-done((bf16[8,16,128]{2,1,0:T(8,128)(2,1)S(1)}, bf16[8,16,128]{2,1,0:T(8,128)(2,1)S(1)}, u32[]{:S(2)}, u32[]{:S(2)}) %collective-permute-start.1) | collective-permute-done | bytes 32800 | tf_op jit(solution)/shard_map/ppermute | solution.py:204
  67.3 0.0 copy-done.2
  67.3 0.0 copy-done
  67.3 0.0 copy-done.1
  67.3 3.5 %neighbour_mean.1 = bf16[8,32,1024]{2,1,0:T(8,128)(2,1)S(1)} custom-call(s32[1025]{0:T(1024)S(1)} %constant_dynamic-update-slice_fusion.plan, bf16[16,8192]{1,0:T(8,128)(2,1)S(1)} %copy-done, s32[256,128]{1,0:T(8,128)S(1)} %copy-done.1, s32[256,128]{1,0:T(8,128)S(1)} %copy-done.2, bf16[256,16,128]{2,1,0:T(8,128)(2,1)S(1)} %bitcast.14, ...), custom_call_target="tpu_custom_call" | custom-call | tf_op jit(solution)/shard_map/neighbour_mean/pallas_call | solution.py:146
  70.7 14.7 %all_to_all.15 = bf16[8,32,1024]{2,1,0:T(8,128)(2,1)S(1)} all-to-all(bf16[8,32,1024]{2,1,0:T(8,128)(2,1)S(1)} %neighbour_mean.1), channel_id=1, replica_groups=mesh['graph'=128,'feat'=8] {'feat'}, dimensions={0} | all-to-all | bytes 1048576 | tf_op jit(solution)/shard_map/all_to_all | solution.py:210
  85.4 0.7 copy-done.8
  86.1 0.3 fusion.1
  86.3 9.9 %all_to_all.16 = bf16[8,16,1024]{2,1,0:T(8,128)(2,1)S(1)} all-to-all(bf16[8,16,1024]{2,1,0:T(8,128)(2,1)S(1)} %bitcast.16), channel_id=1, replica_groups=mesh['graph'=128,'feat'=8] {'feat'}, dimensions={0} | all-to-all | bytes 524288 | tf_op jit(solution)/shard_map/all_to_all | solution.py:211
  96.3 0.7 copy.22
  (14 shorter events, 0.1 us)
Async XLA Ops:
  50.5 5.4 %copy-start.10 = (bf16[8,16,128]{2,1,0:T(8,128)(2,1)S(1)}, bf16[8,16,128]{2,1,0:T(8,128)(2,1)}, u32[]{:S(2)}) copy-start(bf16[8,16,128]{2,1,0:T(8,128)(2,1)} %get-tuple-element.23) | copy-start | bytes 98308
  50.5 8.9 %copy-start.9 = (bf16[8,16,128]{2,1,0:T(8,128)(2,1)S(1)}, bf16[8,16,128]{2,1,0:T(8,128)(2,1)}, u32[]{:S(2)}) copy-start(bf16[8,16,128]{2,1,0:T(8,128)(2,1)} %get-tuple-element.24) | copy-start | bytes 98308
  50.5 11.4 %copy-start.3 = (bf16[128,128]{1,0:T(8,128)(2,1)S(1)}, bf16[128,128]{1,0:T(8,128)(2,1)}, u32[]{:S(2)}) copy-start(bf16[128,128]{1,0:T(8,128)(2,1)} %param.14) | copy-start | bytes 98308
  50.5 11.5 %copy-start.4 = (bf16[128,128]{1,0:T(8,128)(2,1)S(1)}, bf16[128,128]{1,0:T(8,128)(2,1)}, u32[]{:S(2)}) copy-start(bf16[128,128]{1,0:T(8,128)(2,1)} %param.13) | copy-start | bytes 98308
  50.5 12.3 %copy-start.6 = (s32[256]{0:T(256)S(1)}, s32[256]{0:T(256)}, u32[]{:S(2)}) copy-start(s32[256]{0:T(256)} %param.18) | copy-start | bytes 3076
  50.5 12.3 %copy-start.5 = (s32[256]{0:T(256)S(1)}, s32[256]{0:T(256)}, u32[]{:S(2)}) copy-start(s32[256]{0:T(256)} %param.19) | copy-start | bytes 3076
  50.5 12.3 %copy-start.7 = (s32[256]{0:T(256)S(1)}, s32[256]{0:T(256)}, u32[]{:S(2)}) copy-start(s32[256]{0:T(256)} %param.20) | copy-start | bytes 3076
  50.5 16.7 %copy-start.2 = (s32[256,128]{1,0:T(8,128)S(1)}, s32[256,128]{1,0:T(8,128)}, u32[]{:S(2)}) copy-start(s32[256,128]{1,0:T(8,128)} %edge_dst.1) | copy-start | bytes 393220
  50.5 14.8 %all-to-all-start = ((bf16[8,16,2,16,128]{4,3,2,1,0:T(8,128)(2,1)}), bf16[8,16,2,16,128]{4,3,2,1,0:T(8,128)(2,1)S(1)}, u32[]{:S(2)}, u32[]{:S(2)}) async-start(bf16[8,16,2,16,128]{4,3,2,1,0:T(8,128)(2,1)} %broadcast_in_dim.6), calls=%async_computation | async-start | bytes 2097152 | tf_op jit(solution)/shard_map/all_to_all | solution.py:198
  55.8 11.4 %copy-start = (bf16[16,8192]{1,0:T(8,128)(2,1)S(1)}, bf16[16,8192]{1,0:T(8,128)(2,1)}, u32[]{:S(2)}) copy-start(bf16[16,8192]{1,0:T(8,128)(2,1)} %features.3) | copy-start | bytes 786436
  55.8 9.5 %collective-permute-start = (bf16[8,16,128]{2,1,0:T(8,128)(2,1)S(1)}, bf16[8,16,128]{2,1,0:T(8,128)(2,1)S(1)}, u32[]{:S(2)}, u32[]{:S(2)}) collective-permute-start(bf16[8,16,128]{2,1,0:T(8,128)(2,1)S(1)} %copy-done.10), channel_id=1, source_target_pairs={{0,8},{8,16},{16,24},{24,32},{32,40},{40,48},{48,56},{56,64},{64,7... | collective-permute-start | bytes 98312 | tf_op jit(solution)/shard_map/ppermute | solution.py:203
  59.4 7.9 %collective-permute-start.1 = (bf16[8,16,128]{2,1,0:T(8,128)(2,1)S(1)}, bf16[8,16,128]{2,1,0:T(8,128)(2,1)S(1)}, u32[]{:S(2)}, u32[]{:S(2)}) collective-permute-start(bf16[8,16,128]{2,1,0:T(8,128)(2,1)S(1)} %copy-done.9), channel_id=1, source_target_pairs={{8,0},{16,8},{24,16},{32,24},{40,32},{48,40},{56,48},{64,56},{72,6... | collective-permute-start | bytes 98312 | tf_op jit(solution)/shard_map/ppermute | solution.py:204
  62.9 4.4 %copy-start.1 = (s32[256,128]{1,0:T(8,128)S(1)}, s32[256,128]{1,0:T(8,128)}, u32[]{:S(2)}) copy-start(s32[256,128]{1,0:T(8,128)} %edge_src.1) | copy-start | bytes 393220
  85.4 0.7 copy-start.8

commit v6 on v5

--- a/solution.py
+++ b/solution.py
@@ -125,8 +125,7 @@
         degree = jnp.maximum(total[rows : rows + 8], 1.0)
         mean = jnp.concatenate([total[r : r + 8] / degree for r in range(0, rows, 8)], axis=0)
         at = (b % per) * BLOCK
-        shares[b // per, :rows, at : at + BLOCK] = table[b]
-        shares[b // per, rows:, at : at + BLOCK] = mean.astype(shares.dtype)
+        shares[b // per, :, at : at + BLOCK] = mean.astype(shares.dtype)
 
 
 def neighbour_mean(
@@ -145,7 +144,7 @@
     vmem = pl.BlockSpec(memory_space=pltpu.VMEM)
     return pl.pallas_call(
         mean_kernel,
-        out_shape=jax.ShapeDtypeStruct((parts, 2 * rows, nodes // parts), features.dtype),
+        out_shape=jax.ShapeDtypeStruct((parts, rows, nodes // parts), features.dtype),
         in_specs=[smem] + [vmem] * 6,
         out_specs=vmem,
         scratch_shapes=[
@@ -188,8 +187,8 @@
         [X * (z + r) + x for r in range(STRIDE) for x in range(X)] for z in range(0, Z, STRIDE)
     ]
     column = lax.all_gather(hub_local, "graph", axis_index_groups=along_z)
-    column, tile_src, tile_edges, w_self, w_neigh = lax.optimization_barrier(
-        (column, tile_src, tile_edges, w_self, w_neigh)
+    column, features, tile_src, tile_edges, w_self, w_neigh = lax.optimization_barrier(
+        (column, features, tile_src, tile_edges, w_self, w_neigh)
     )
     weights = jnp.stack(
         [w_self.reshape(-1, parts, rows), w_neigh.reshape(-1, parts, rows)], axis=2
@@ -203,11 +202,12 @@
     halo_low = lax.ppermute(to_next, "graph", forward)
     halo_high = lax.ppermute(to_previous, "graph", backward)
 
-    hub_rows, weights = lax.optimization_barrier((hub_rows, weights))
+    split = jnp.transpose(features.reshape(rows, parts, nodes // parts), (1, 0, 2))
+    hub_rows, weights, split = lax.optimization_barrier((hub_rows, weights, split))
     shares = neighbour_mean(
         features, hub_rows, halo_low, halo_high, tile_dst, tile_src, tile_edges, tile_count, edge_src, edge_dst, parts
     )
-    shares = lax.all_to_all(shares, "feat", 0, 0)
+    shares = lax.all_to_all(jnp.concatenate([split, shares], axis=1), "feat", 0, 0)
     updated = lax.all_to_all(project(shares, weights, bias), "feat", 0, 0)
     return jnp.transpose(updated, (1, 0, 2)).reshape(rows, nodes)
 

time: 97.4 us -> 97.8 us (level)
  no operation moved by 1% of the time
where the time goes in v6:
time: 97.8 us; the launch traced here: 97 us
  blocking collectives  72.3 us (74%)
  starting transfers between devices  11.3 us (12%)
  Pallas kernels  5.02 us (5%)
  waiting for transfers between devices  4.31 us (4%)
  local copies, waits for them, and re-layouts  2.84 us (3%)
    all_gather x1, blocking collectives, shards(): column = lax.all_gather(hub_local, 'graph', axis_index_groups=along_z)  47.7 us
    all_to_all x1, blocking collectives, shards(): lax.all_to_all(jnp.concatenate([split, shares], axis=1), 'feat', 0, 0)  14.7 us
    all_to_all x1, blocking collectives, shards(): updated = lax.all_to_all(project(shares, weights, bias), 'feat', 0, 0)  9.95 us
    all_to_all x1, starting transfers between devices, shards(): hub_rows = lax.all_to_all(spread, 'graph', 0, 0, axis_index_groups=nearby)  5.29 us
    ppermute x1, starting transfers between devices, shards(): halo_low = lax.ppermute(to_next, 'graph', forward)  3.5 us
    pallas_call x1, Pallas kernels, neighbour_mean(): pl.pallas_call(mean_kernel, out_shape=jax.ShapeDtypeStruct((parts, rows,...  3.42 us
    ppermute x1, starting transfers between devices, shards(): halo_high = lax.ppermute(to_previous, 'graph', backward)  2.47 us
    all_to_all x1, waiting for transfers between devices, shards(): hub_rows = lax.all_to_all(spread, 'graph', 0, 0, axis_index_groups=nearby)  2.4 us
  transfers between devices with their start and end apart: 3, of which 2 were waited for; matrix products, arithmetic and copies ran while one was open for 0% of the time, Pallas kernels for 0%

profile of v6, /device:TPU:6, one launch (start us, length us, event | category | flops | bytes accessed | tf_op | source)
XLA Modules:
  0.0 97.0 jit_solution(8631711688974323489)
XLA Ops:
  0.0 1.6 %pick_blocks.1 = (bf16[2,16,128]{2,1,0:T(8,128)(2,1)}, bf16[8,16,128]{2,1,0:T(8,128)(2,1)}, bf16[8,16,128]{2,1,0:T(8,128)(2,1)}) custom-call(s32[2]{0:T(128)} %hub_pick.1, s32[16]{0:T(128)} %halo_send.1, bf16[16,8192]{1,0:T(8,128)(2,1)} %features.2), custom_call_target="tpu_custom_call" | custom-call | tf_op jit(solution)/shard_map/pick_blocks/pallas_call | solution.py:29
  1.6 47.7 %all-gather = bf16[32,16,128]{2,1,0:T(8,128)(2,1)S(1)} all-gather(bf16[2,16,128]{2,1,0:T(8,128)(2,1)} %get-tuple-element.17), channel_id=2, replica_groups={{0,64,128,192,256,320,384,448,512,576,640,704,768,832,896,960},{8,72,13..., dimensions={0}, use_global_device_ids=true | all-gather | bytes 139264 | tf_op jit(solution)/shard_map/all_gather | solution.py:189
  49.3 1.2 %broadcast_in_dim.6 = bf16[8,16,2,16,128]{4,3,2,1,0:T(8,128)(2,1)} broadcast(bf16[16,2,16,128]{3,2,1,0:T(8,128)(2,1)S(1)} %bitcast.27), dimensions={1,2,3,4} | broadcast | bytes 1179648 | tf_op jit(solution)/shard_map/broadcast_in_dim | solution.py:196
  50.5 0.0 copy-start.6
  50.5 0.0 copy-start.5
  50.5 0.0 copy-start.7
  50.5 5.3 %all-to-all-start = ((bf16[8,16,2,16,128]{4,3,2,1,0:T(8,128)(2,1)}), bf16[8,16,2,16,128]{4,3,2,1,0:T(8,128)(2,1)S(1)}, u32[]{:S(2)}, u32[]{:S(2)}) async-start(bf16[8,16,2,16,128]{4,3,2,1,0:T(8,128)(2,1)} %broadcast_in_dim.6), calls=%async_computation | async-start | bytes 2097152 | tf_op jit(solution)/shard_map/all_to_all | solution.py:197
  55.8 0.0 copy-done.10
  55.8 3.5 %collective-permute-start = (bf16[8,16,128]{2,1,0:T(8,128)(2,1)S(1)}, bf16[8,16,128]{2,1,0:T(8,128)(2,1)S(1)}, u32[]{:S(2)}, u32[]{:S(2)}) collective-permute-start(bf16[8,16,128]{2,1,0:T(8,128)(2,1)S(1)} %copy-done.10), channel_id=1, source_target_pairs={{0,8},{8,16},{16,24},{24,32},{32,40},{40,48},{48,56},{56,64},{64,7... | collective-permute-start | bytes 98312 | tf_op jit(solution)/shard_map/ppermute | solution.py:202
  59.3 0.0 copy-done.9
  59.3 2.5 %collective-permute-start.1 = (bf16[8,16,128]{2,1,0:T(8,128)(2,1)S(1)}, bf16[8,16,128]{2,1,0:T(8,128)(2,1)S(1)}, u32[]{:S(2)}, u32[]{:S(2)}) collective-permute-start(bf16[8,16,128]{2,1,0:T(8,128)(2,1)S(1)} %copy-done.9), channel_id=1, source_target_pairs={{8,0},{16,8},{24,16},{32,24},{40,32},{48,40},{56,48},{64,56},{72,6... | collective-permute-start | bytes 98312 | tf_op jit(solution)/shard_map/ppermute | solution.py:203
  61.8 0.0 copy-done.3
  61.8 0.1 copy.20
  62.0 0.0 copy-done.4
  62.0 0.1 copy.19
  62.7 0.0 copy-done.6
  62.8 0.0 copy-done.5
  62.8 0.0 copy-done.7
  62.9 0.0 copy-done
  62.9 0.0 copy-start.1
  62.9 0.0 copy-start.2
  62.9 2.4 %all-to-all-done = bf16[8,16,2,16,128]{4,3,2,1,0:T(8,128)(2,1)S(1)} async-done(((bf16[8,16,2,16,128]{4,3,2,1,0:T(8,128)(2,1)}), bf16[8,16,2,16,128]{4,3,2,1,0:T(8,128)(2,1)S(1)}, u32[]{:S(2)}, u32[]{:S(2)}) %all-to-all-start) | async-done | bytes 1048608 | tf_op jit(solution)/shard_map/all_to_all | solution.py:197
  65.3 0.0 collective-permute-done.halo_low
  65.3 1.9 %collective-permute-done.1.halo_high = bf16[8,16,128]{2,1,0:T(8,128)(2,1)S(1)} collective-permute-done((bf16[8,16,128]{2,1,0:T(8,128)(2,1)S(1)}, bf16[8,16,128]{2,1,0:T(8,128)(2,1)S(1)}, u32[]{:S(2)}, u32[]{:S(2)}) %collective-permute-start.1) | collective-permute-done | bytes 32800 | tf_op jit(solution)/shard_map/ppermute | solution.py:203
  67.3 0.0 copy-done.1
  67.3 0.0 copy-done.2
  67.3 3.4 %neighbour_mean.1 = bf16[8,16,1024]{2,1,0:T(8,128)(2,1)S(1)} custom-call(s32[1025]{0:T(1024)S(1)} %constant_dynamic-update-slice_fusion.plan, bf16[16,8192]{1,0:T(8,128)(2,1)S(1)} %copy-done, s32[256,128]{1,0:T(8,128)S(1)} %copy-done.1, s32[256,128]{1,0:T(8,128)S(1)} %copy-done.2, bf16[256,16,128]{2,1,0:T(8,128)(2,1)S(1)} %bitcast.21, ...), custom_call_target="tpu_custom_call" | custom-call | tf_op jit(solution)/shard_map/neighbour_mean/pallas_call | solution.py:145
  70.7 14.7 %all_to_all.15 = bf16[8,32,1024]{2,1,0:T(8,128)(2,1)S(1)} all-to-all(bf16[8,32,1024]{2,1,0:T(8,128)(2,1)S(1)} %pad_maximum_fusion), channel_id=1, replica_groups=mesh['graph'=128,'feat'=8] {'feat'}, dimensions={0} | all-to-all | bytes 1048576 | tf_op jit(solution)/shard_map/all_to_all | solution.py:210
  85.4 0.7 copy-done.8
  86.1 0.3 fusion.1
  86.3 9.9 %all_to_all.16 = bf16[8,16,1024]{2,1,0:T(8,128)(2,1)S(1)} all-to-all(bf16[8,16,1024]{2,1,0:T(8,128)(2,1)S(1)} %bitcast.24), channel_id=1, replica_groups=mesh['graph'=128,'feat'=8] {'feat'}, dimensions={0} | all-to-all | bytes 524288 | tf_op jit(solution)/shard_map/all_to_all | solution.py:211
  96.3 0.7 copy.25
  (16 shorter events, 0.1 us)
Async XLA Ops:
  50.5 5.3 %copy-start.10 = (bf16[8,16,128]{2,1,0:T(8,128)(2,1)S(1)}, bf16[8,16,128]{2,1,0:T(8,128)(2,1)}, u32[]{:S(2)}) copy-start(bf16[8,16,128]{2,1,0:T(8,128)(2,1)} %get-tuple-element.27) | copy-start | bytes 98308
  50.5 8.8 %copy-start.9 = (bf16[8,16,128]{2,1,0:T(8,128)(2,1)S(1)}, bf16[8,16,128]{2,1,0:T(8,128)(2,1)}, u32[]{:S(2)}) copy-start(bf16[8,16,128]{2,1,0:T(8,128)(2,1)} %get-tuple-element.28) | copy-start | bytes 98308
  50.5 11.3 %copy-start.3 = (bf16[128,128]{1,0:T(8,128)(2,1)S(1)}, bf16[128,128]{1,0:T(8,128)(2,1)}, u32[]{:S(2)}) copy-start(bf16[128,128]{1,0:T(8,128)(2,1)} %param.14) | copy-start | bytes 98308
  50.5 11.5 %copy-start.4 = (bf16[128,128]{1,0:T(8,128)(2,1)S(1)}, bf16[128,128]{1,0:T(8,128)(2,1)}, u32[]{:S(2)}) copy-start(bf16[128,128]{1,0:T(8,128)(2,1)} %param.13) | copy-start | bytes 98308
  50.5 12.3 %copy-start.6 = (s32[256]{0:T(256)S(1)}, s32[256]{0:T(256)}, u32[]{:S(2)}) copy-start(s32[256]{0:T(256)} %param.18) | copy-start | bytes 3076
  50.5 12.3 %copy-start.5 = (s32[256]{0:T(256)S(1)}, s32[256]{0:T(256)}, u32[]{:S(2)}) copy-start(s32[256]{0:T(256)} %param.19) | copy-start | bytes 3076
  50.5 12.3 %copy-start.7 = (s32[256]{0:T(256)S(1)}, s32[256]{0:T(256)}, u32[]{:S(2)}) copy-start(s32[256]{0:T(256)} %param.20) | copy-start | bytes 3076
  50.5 14.8 %all-to-all-start = ((bf16[8,16,2,16,128]{4,3,2,1,0:T(8,128)(2,1)}), bf16[8,16,2,16,128]{4,3,2,1,0:T(8,128)(2,1)S(1)}, u32[]{:S(2)}, u32[]{:S(2)}) async-start(bf16[8,16,2,16,128]{4,3,2,1,0:T(8,128)(2,1)} %broadcast_in_dim.6), calls=%async_computation | async-start | bytes 2097152 | tf_op jit(solution)/shard_map/all_to_all | solution.py:197
  55.8 7.1 %copy-start = (bf16[16,8192]{1,0:T(8,128)(2,1)S(1)}, bf16[16,8192]{1,0:T(8,128)(2,1)}, u32[]{:S(2)}) copy-start(bf16[16,8192]{1,0:T(8,128)(2,1)} %features.2) | copy-start | bytes 786436
  55.8 9.5 %collective-permute-start = (bf16[8,16,128]{2,1,0:T(8,128)(2,1)S(1)}, bf16[8,16,128]{2,1,0:T(8,128)(2,1)S(1)}, u32[]{:S(2)}, u32[]{:S(2)}) collective-permute-start(bf16[8,16,128]{2,1,0:T(8,128)(2,1)S(1)} %copy-done.10), channel_id=1, source_target_pairs={{0,8},{8,16},{16,24},{24,32},{32,40},{40,48},{48,56},{56,64},{64,7... | collective-permute-start | bytes 98312 | tf_op jit(solution)/shard_map/ppermute | solution.py:202
  59.3 7.9 %collective-permute-start.1 = (bf16[8,16,128]{2,1,0:T(8,128)(2,1)S(1)}, bf16[8,16,128]{2,1,0:T(8,128)(2,1)S(1)}, u32[]{:S(2)}, u32[]{:S(2)}) collective-permute-start(bf16[8,16,128]{2,1,0:T(8,128)(2,1)S(1)} %copy-done.9), channel_id=1, source_target_pairs={{8,0},{16,8},{24,16},{32,24},{40,32},{48,40},{56,48},{64,56},{72,6... | collective-permute-start | bytes 98312 | tf_op jit(solution)/shard_map/ppermute | solution.py:203
  62.9 4.4 %copy-start.1 = (s32[256,128]{1,0:T(8,128)S(1)}, s32[256,128]{1,0:T(8,128)}, u32[]{:S(2)}) copy-start(s32[256,128]{1,0:T(8,128)} %edge_src.1) | copy-start | bytes 393220
  62.9 4.4 %copy-start.2 = (s32[256,128]{1,0:T(8,128)S(1)}, s32[256,128]{1,0:T(8,128)}, u32[]{:S(2)}) copy-start(s32[256,128]{1,0:T(8,128)} %edge_dst.1) | copy-start | bytes 393220
  85.4 0.7 copy-start.8
